TPU v7x, 32 devices: a whole 2x2x4 slice. The times are simulated.
32 devices in a mesh: section: 4 (over z), dp: 8 (over y, x, core).
Axes of the slice: x: 2, y: 2, z: 4, core: 2. Of those that a mesh axis runs over, the one named last changes fastest.
Arguments:
- inputs: bfloat16 [4, 256, 6144], P(None, 'dp', 'section'), may hold values from -6 to 6
- gain: float32 [4, 6144], P('section'), may hold values from 0.1 to 1.9
- repeats: int32 [4], P('section'), may hold values from 0 to 3
- order: int32 [4], replicated, may hold values from 0 to 3, each once
- hidden_grad: bfloat16 [4, 4, 256, 12288], P('section', None, 'dp'), may hold values from -6 to 6
Outputs:
- feature_factor: float32 [4, 3072, 128], P('section', 'dp')
- hidden_factor: float32 [4, 12288, 128], P('section', 'dp')
Inputs may be any that keep to these rules, and one draw needn't show every extreme that they name: `order`: each micro-batch id once.
All inputs are finite; a program needn't handle non-finite values.
Results may differ from a plain program's by a relative error of at most 0.0085.
Values may be sent and summed in bfloat16 or wider, within the bound.
No kernel may reach another device: no remote copies, remote signals or barrier semaphores. Data moves between devices by JAX's collectives and lax.ppermute only.
A program may use at most 128 MiB of HBM per device.

v0:
```python
import functools

import jax
import jax.numpy as jnp
from jax import lax
from jax.experimental import pallas as pl
from jax.experimental.pallas import tpu as pltpu
from jax.sharding import PartitionSpec as P

AWIN = 3072
GWIN = 12288
BLK = 128
VMEM_LIMIT = 16 * 1024 * 1024
ROOT = 0.7978845608028654

SMEM_SPEC = pl.BlockSpec(memory_space=pltpu.SMEM)
VMEM_SPEC = pl.BlockSpec(memory_space=pltpu.VMEM)


def params(limit=VMEM_LIMIT):
    return pltpu.CompilerParams(vmem_limit_bytes=limit)


def gelu(x):
    inner = ROOT * (x + 0.044715 * (x * x * x))
    return x * (0.5 * (1.0 + jnp.tanh(inner)))


def batch_weight(order_ref, batch_id, micro):
    weight = jnp.float32(0.0)
    for slot in range(micro):
        weight = jnp.where(order_ref[slot] == batch_id, jnp.float32(0.5 * 0.5 ** (micro - 1 - slot)), weight)
    return weight


def gram(left, right):
    return lax.dot_general(left, right, (((0,), (0,)), ((), ())), preferred_element_type=jnp.float32)


def iotas():
    row = lax.broadcasted_iota(jnp.int32, (BLK, BLK), 0)
    col = lax.broadcasted_iota(jnp.int32, (BLK, BLK), 1)
    return row, col


def packed_rows(pairs):
    return pairs * BLK + -(-pairs // 16) * 16


def hidden_kernel(micro, pairs, scale, order_ref, _, *refs):
    grad_refs, out_ref = refs[:-1], refs[-1]
    row, col = iotas()
    weights = [batch_weight(order_ref, m, micro) for m in range(micro)]
    tail_row = lax.broadcasted_iota(jnp.int32, (packed_rows(pairs) - pairs * BLK, BLK), 0)
    for place, grad_ref in enumerate(grad_refs):
        for half in range(2):
            tail = jnp.zeros(tail_row.shape, jnp.float32)
            for pair in range(pairs):
                at = (half * pairs + pair) * 2 * BLK
                parts = [grad_ref[0, m, :, at:at + 2 * BLK] for m in range(micro)]
                scaled = [(part.astype(jnp.float32) * weight).astype(jnp.bfloat16) for part, weight in zip(parts, weights)]
                both = gram(jnp.concatenate(scaled, axis=0), jnp.concatenate(parts, axis=0)) * scale
                first, second = both[:BLK, :BLK], both[BLK:, BLK:]
                packed = jnp.where(col >= row, first, second).astype(jnp.bfloat16)
                out_ref[place, half, pair * BLK:(pair + 1) * BLK] = packed
                diagonal = jnp.sum(jnp.where(col == row, second, 0.0), axis=0, keepdims=True)
                tail = jnp.where(tail_row == pair, diagonal, tail)
            out_ref[place, half, pairs * BLK:] = tail.astype(jnp.bfloat16)


def hidden_terms(order, hidden_grad, me, dp_count, scale, cost):
    _, micro, rows, width = hidden_grad.shape
    own = width // dp_count
    pairs = own // (4 * BLK)
    shape, count = (2, packed_rows(pairs), BLK), dp_count // 2

    def owner(flip):
        return lambda i, order, me: (0, 0, 0, jnp.bitwise_xor(me[0], 2 - 2 * i + flip))

    return pl.pallas_call(
        functools.partial(hidden_kernel, micro, pairs, scale),
        out_shape=jax.ShapeDtypeStruct((count,) + shape, jnp.bfloat16),
        grid_spec=pltpu.PrefetchScalarGridSpec(
            num_scalar_prefetch=2,
            grid=(count // 2,),
            in_specs=[pl.BlockSpec((1, micro, rows, own), owner(4)), pl.BlockSpec((1, micro, rows, own), owner(0))],
            out_specs=pl.BlockSpec((2,) + shape, lambda i, order, me: (i, 0, 0, 0)),
        ),
        compiler_params=params(),
        cost_estimate=pl.CostEstimate(flops=cost, bytes_accessed=1 << 10, transcendentals=0),
    )(order, me, hidden_grad, hidden_grad)


def small_call(kernel, shapes, *operands, cost=1 << 20):
    return pl.pallas_call(
        kernel,
        out_shape=shapes,
        in_specs=[VMEM_SPEC] * len(operands),
        out_specs=jax.tree.map(lambda _: VMEM_SPEC, shapes),
        compiler_params=params(),
        cost_estimate=pl.CostEstimate(flops=cost, bytes_accessed=1 << 10, transcendentals=0),
    )(*operands)


def core_sum_kernel(near_ref, came_ref, along_x_ref, along_y_ref, first_ref, second_ref):
    def total(place, half):
        return near_ref[place, half].astype(jnp.float32) + came_ref[place, half].astype(jnp.float32)

    for i in range(2):
        along_x_ref[i] = total(i, 0).astype(jnp.bfloat16)
        along_y_ref[i] = total(2 * i, 1).astype(jnp.bfloat16)
        first_ref[i] = total(2 + i, 0)
        second_ref[i] = total(1 + 2 * i, 1)


def pair_sum_kernel(first_ref, came_x_ref, second_ref, came_y_ref, along_y_ref, along_x_ref, kept_ref):
    along_y_ref[...] = (first_ref[0] + came_x_ref[0].astype(jnp.float32)).astype(jnp.bfloat16)
    along_x_ref[...] = (second_ref[0] + came_y_ref[0].astype(jnp.float32)).astype(jnp.bfloat16)
    kept_ref[0] = first_ref[1] + came_x_ref[1].astype(jnp.float32)
    kept_ref[1] = second_ref[1] + came_y_ref[1].astype(jnp.float32)


def unpack_kernel(pairs, kept_ref, came_y_ref, came_x_ref, out_ref):
    row, col = iotas()
    for half, came_ref in enumerate((came_y_ref, came_x_ref)):

        def total(rows):
            return kept_ref[half, rows] + came_ref[rows].astype(jnp.float32)

        tail = total(slice(pairs * BLK, None))
        for pair in range(pairs):
            value = total(slice(pair * BLK, (pair + 1) * BLK))
            turned = value.T
            at = (half * pairs + pair) * 2 * BLK
            out_ref[0, at:at + BLK] = jnp.where(col >= row, value, turned)
            second = jnp.where(col == row, tail[pair:pair + 1], turned)
            out_ref[0, at + BLK:at + 2 * BLK] = jnp.where(col < row, value, second)


def core_sum(near, came):
    one = near.shape[2:]
    sent = jax.ShapeDtypeStruct((2,) + one, jnp.bfloat16)
    kept = jax.ShapeDtypeStruct((2,) + one, jnp.float32)
    return small_call(core_sum_kernel, (sent, sent, kept, kept), near, came)


def pair_sum(first, came_x, second, came_y):
    last = jax.ShapeDtypeStruct(first.shape[1:], jnp.bfloat16)
    return small_call(pair_sum_kernel, (last, last, first), first, came_x, second, came_y)


def unpacked(kept, came_y, came_x):
    pairs = kept.shape[1] // BLK
    out = jax.ShapeDtypeStruct((1, 4 * pairs * BLK, BLK), jnp.float32)
    return small_call(functools.partial(unpack_kernel, pairs), out, kept, came_y, came_x)


def swapped(shard, axis, mask):
    return lax.ppermute(shard, axis, [(i, i ^ mask) for i in range(lax.axis_size(axis))])


def message_kernel(in_ref, gain_ref, repeats_ref, me_ref, *out_refs):
    _, rows, part = in_ref.shape
    chunks, gain_rows = part // BLK, gain_ref.shape[0]
    gain = gain_ref[...]
    high = gain.astype(jnp.bfloat16)
    low = (gain - high.astype(jnp.float32)).astype(jnp.bfloat16)
    count = jnp.full((16, BLK), repeats_ref[0], jnp.int32).astype(jnp.float32).astype(jnp.bfloat16)
    at = chunks * rows
    for mask, out_ref in enumerate(out_refs, 1):
        target = jnp.bitwise_xor(me_ref[0], mask)
        for chunk in range(chunks):
            out_ref[chunk * rows:(chunk + 1) * rows] = in_ref[target, :, chunk * BLK:(chunk + 1) * BLK]
        out_ref[at:at + gain_rows] = high
        out_ref[at + gain_rows:at + 2 * gain_rows] = low
        out_ref[at + 2 * gain_rows:] = count


def messages(inputs, gain, repeats, me):
    micro, rows, part = inputs.shape
    shape = jax.ShapeDtypeStruct((part // BLK * rows + 2 * gain.shape[0] + 16, BLK), jnp.bfloat16)
    return pl.pallas_call(
        message_kernel,
        out_shape=(shape,) * (micro - 1),
        in_specs=[VMEM_SPEC, VMEM_SPEC, SMEM_SPEC, SMEM_SPEC],
        out_specs=(VMEM_SPEC,) * (micro - 1),
        compiler_params=params(),
        cost_estimate=pl.CostEstimate(flops=1 << 33, bytes_accessed=1 << 20, transcendentals=0),
    )(inputs, gain, repeats, me)


def relay_kernel(sections, owners, own_ref, gain_ref, repeats_ref, me_ref, *refs):
    received, out_refs, (held, gains) = refs[:sections - 1], refs[sections - 1:-2], refs[-2:]
    chunks, rows, _ = held.shape
    own = AWIN // owners // BLK
    width = chunks * BLK
    part = chunks // sections
    at = part * rows
    me = me_ref[0]
    none = jnp.zeros((rows, BLK), jnp.float32)

    def mean(total):
        return jnp.sum(total, axis=-1, keepdims=True) * (1.0 / width)

    gains[me, :chunks] = gain_ref[...]
    gains[me, chunks:] = jnp.full((8, BLK), repeats_ref[0], jnp.int32).astype(jnp.float32)
    total = none
    for chunk in range(part):
        value = own_ref[me, :, chunk * BLK:(chunk + 1) * BLK].astype(jnp.float32)
        held[me * part + chunk] = value
        total = total + value
    for mask, ref in enumerate(received, 1):
        source = jnp.bitwise_xor(me, mask)
        gains[source, :chunks] = ref[at:at + chunks].astype(jnp.float32) + ref[at + chunks:at + 2 * chunks].astype(jnp.float32)
        gains[source, chunks:] = ref[at + 2 * chunks:].astype(jnp.float32)[:8]
        for chunk in range(part):
            value = ref[chunk * rows:(chunk + 1) * rows].astype(jnp.float32)
            held[source * part + chunk] = value
            total = total + value
    center = mean(total)
    square = none
    for chunk in range(chunks):
        square = square + jnp.square(held[chunk] - center)
    start = (center, lax.rsqrt(mean(square) + 1e-05))

    def section(s, carry):
        repeats = jnp.max(gains[s, chunks:]).astype(jnp.int32)

        def apply(_, carry):
            center, scale = carry
            half = 0.5 * scale
            total, square = none, none
            for chunk in range(chunks):
                value = held[chunk]
                y = (value - center) * half * gains[s, chunk:chunk + 1]
                inner = y * (2.0 * ROOT + (8.0 * 0.044715 * ROOT) * (y * y))
                value = (value + (y + y * jnp.tanh(inner))).astype(jnp.bfloat16).astype(jnp.float32)
                held[chunk] = value
                moved = value - center
                total = total + moved
                square = square + moved * moved
            shift = mean(total)
            spread = jnp.maximum(mean(square) - shift * shift, 0.0)
            return center + shift, lax.rsqrt(spread + 1e-05)

        carry = lax.fori_loop(0, repeats + 1, apply, carry)
        center, scale = carry
        for mask, out_ref in enumerate(out_refs):
            place = jnp.bitwise_xor(me_ref[1], mask) * own
            for i in range(own):
                normed = (held[place + i] - center) * scale * gains[s, pl.ds(place + i, 1)]
                out_ref[s, :, i * BLK:(i + 1) * BLK] = normed.astype(jnp.bfloat16)
        return carry

    lax.fori_loop(0, sections, section, start)


def relay(inputs, gain, repeats, me, received, owners):
    sections, rows, part = inputs.shape
    chunks = sections * part // BLK
    shape = jax.ShapeDtypeStruct((sections, rows, AWIN // owners), jnp.bfloat16)
    return pl.pallas_call(
        functools.partial(relay_kernel, sections, owners),
        out_shape=(shape,) * owners,
        in_specs=[VMEM_SPEC, VMEM_SPEC, SMEM_SPEC, SMEM_SPEC] + [VMEM_SPEC] * len(received),
        out_specs=(VMEM_SPEC,) * owners,
        scratch_shapes=[pltpu.VMEM((chunks, rows, BLK), jnp.float32), pltpu.VMEM((sections, chunks + 8, BLK), jnp.float32)],
        compiler_params=params(),
        cost_estimate=pl.CostEstimate(flops=1 << 33, bytes_accessed=2 << 20, transcendentals=0),
    )(inputs, gain, repeats, me, *received)


HALF = BLK // 2
FEATURE_ROWS = BLK + HALF + 16


def pack_three(first, second, third):
    row, col = iotas()
    low_row, low_col = row[:HALF], col[:HALF]
    turned = pltpu.roll(third[HALF:], HALF, 1)
    two = jnp.where(col >= row, first, second)
    half = jnp.where(low_col < low_row, turned, third[:HALF])
    tail_row = lax.broadcasted_iota(jnp.int32, (16, BLK), 0)
    diagonal = jnp.sum(jnp.where(col == row, second, 0.0), axis=0, keepdims=True)
    last = jnp.sum(jnp.where(low_col == low_row + HALF, third[HALF:], 0.0), axis=0, keepdims=True)
    tail = jnp.where(tail_row == 0, diagonal, jnp.where(tail_row == 1, last, 0.0))
    return jnp.concatenate([two, half, tail], axis=0)


def unpack_three(packed):
    row, col = iotas()
    low_row, low_col = row[:HALF], col[:HALF]
    two, half, tail = packed[:BLK], packed[BLK:BLK + HALF], packed[BLK + HALF:]
    turned = two.T
    first = jnp.where(col >= row, two, turned)
    second = jnp.where(col < row, two, jnp.where(col == row, tail[0:1], turned))
    across = jnp.concatenate([half, jnp.zeros_like(half)], axis=0).T
    upper = jnp.where(low_col < low_row, across[:HALF], half)
    corner = pltpu.roll(jnp.where(low_col < low_row, half, across[:HALF]), HALF, 1)
    lower = jnp.where(low_col < HALF, across[HALF:], jnp.where(low_col == low_row + HALF, tail[1:2], corner))
    return jnp.concatenate([first, second, upper, lower], axis=0)


def feature_kernel(micro, scale, order_ref, me_ref, *refs):
    in_refs, (own_ref, *out_refs) = refs[:-micro], refs[-micro:]
    weight = batch_weight(order_ref, me_ref[0], micro) * scale
    for mask, out_ref in enumerate([own_ref] + out_refs):
        s = jnp.bitwise_xor(me_ref[0], mask)
        blocks = []
        for at in range(0, 3 * BLK, BLK):
            feats = jnp.concatenate([ref[s, :, at:at + BLK] for ref in in_refs], axis=0)
            blocks.append(gram(feats, feats) * weight)
        out_ref[...] = pack_three(*blocks).astype(out_ref.dtype)


def feature_terms(order, me, feats, micro, scale):
    return pl.pallas_call(
        functools.partial(feature_kernel, micro, scale),
        out_shape=(jax.ShapeDtypeStruct((FEATURE_ROWS, BLK), jnp.float32),)
        + (jax.ShapeDtypeStruct((FEATURE_ROWS, BLK), jnp.bfloat16),) * (micro - 1),
        in_specs=[SMEM_SPEC, SMEM_SPEC] + [VMEM_SPEC] * len(feats),
        out_specs=(VMEM_SPEC,) * micro,
        compiler_params=params(),
        cost_estimate=pl.CostEstimate(flops=1 << 31, bytes_accessed=1 << 20, transcendentals=0),
    )(order, me, *feats)


def feature_sum_kernel(*refs):
    total = refs[0][...]
    for ref in refs[1:-1]:
        total = total + ref[...].astype(jnp.float32)
    refs[-1][0] = unpack_three(total)


def fast_body(inputs, gain, repeats, order, hidden_grad):
    micro, tok_rows, _ = inputs.shape
    dp_count = lax.axis_size("dp")
    scale = 1.0 / (tok_rows * dp_count)
    gain = gain.reshape(-1, BLK)
    plane, place = lax.axis_index("section").reshape(1), lax.axis_index("dp").reshape(1)
    me = jnp.concatenate([plane, place])
    told, order = lax.optimization_barrier((messages(inputs, gain, repeats, plane), order))
    pieces = {mask: swapped(told[mask - 1], "section", mask) for mask in (2, 3, 1)}
    pieces = tuple(pieces[mask] for mask in (1, 2, 3))

    came = swapped(hidden_terms(order, hidden_grad, place ^ 1, dp_count, scale, 1 << 20), "dp", 1)
    near = hidden_terms(order, hidden_grad, place, dp_count, scale, 1 << 34)
    along_x, along_y, first, second = core_sum(near, came)
    came_x, came_y = swapped(along_x, "dp", 2), swapped(along_y, "dp", 4)
    pieces, first = lax.optimization_barrier((pieces, first))

    feats = relay(inputs, gain, repeats, me, pieces, dp_count)
    feats, came_x, came_y = lax.optimization_barrier((feats, came_x, came_y))
    gathered = [feats[0]] + [swapped(feats[mask], "dp", mask) for mask in (6, 7, 4, 2, 5, 3, 1)]
    own, *terms = feature_terms(order, plane, gathered, micro, scale)
    terms = [swapped(terms[mask - 1], "section", mask) for mask in (2, 3, 1)]
    own, first = lax.optimization_barrier((own, first))
    along_y, along_x, kept = pair_sum(first, came_x, second, came_y)
    came_y, came_x = swapped(along_y, "dp", 4), swapped(along_x, "dp", 2)
    feature_rows = small_call(feature_sum_kernel, jax.ShapeDtypeStruct((1, 3 * BLK, BLK), jnp.float32), own, *terms, cost=1 << 34)
    kept, feature_rows = lax.optimization_barrier((kept, feature_rows))
    hidden_rows = unpacked(kept, came_y, came_x)
    return (feature_rows, hidden_rows)


def normed(value, gain_row):
    center = jnp.mean(value, axis=-1, keepdims=True)
    spread = jnp.mean(jnp.square(value - center), axis=-1, keepdims=True)
    return (value - center) * lax.rsqrt(spread + 1e-05) * gain_row


def weighted_gram(feats, weights):
    shaped = feats.reshape(feats.shape[0], -1, BLK)
    scaled = shaped * weights[:, None, None].astype(shaped.dtype)
    return jnp.einsum("tbi,tbj->bij", scaled, shaped, preferred_element_type=jnp.float32)


def plain_body(inputs, gain, repeats, order, hidden_grad):
    micro, tok_rows, part = inputs.shape
    sections = lax.axis_size("section")
    total_tok = tok_rows * lax.axis_size("dp")
    slot_weight = 0.5 * jnp.power(0.5, micro - 1 - jnp.arange(micro, dtype=jnp.float32))
    hidden_weight = jnp.zeros((micro,), jnp.float32).at[order].set(slot_weight)
    row_weight = jnp.repeat(hidden_weight, tok_rows)
    hidden = weighted_gram(hidden_grad.reshape(micro * tok_rows, GWIN), row_weight) / total_tok
    gains = lax.all_gather(gain[0], "section", axis=0)
    counts = lax.all_gather(repeats[0], "section", axis=0)
    pieces = lax.all_to_all(inputs.reshape(micro * tok_rows, part), "section", 0, 1, tiled=True)

    def section(s, carry):
        value, feats = carry
        value = lax.fori_loop(
            0,
            counts[s] + 1,
            lambda i, v: (v + gelu(normed(v, gains[s]))).astype(jnp.bfloat16).astype(jnp.float32),
            value,
        )
        now = normed(value, gains[s]).astype(jnp.bfloat16)[:, :AWIN]
        return value, lax.dynamic_update_index_in_dim(feats, now, s, 0)

    start = jnp.zeros((sections, pieces.shape[0], AWIN), jnp.bfloat16)
    _, feats = lax.fori_loop(0, sections, section, (pieces.astype(jnp.float32), start))
    feats = lax.all_to_all(feats, "section", 0, 0, tiled=True).reshape(micro * tok_rows, AWIN)
    feature = weighted_gram(feats, row_weight) / total_tok

    def shared(term):
        term = term.reshape(-1, BLK).astype(jnp.bfloat16)
        return lax.psum_scatter(term, "dp", scatter_dimension=0, tiled=True).astype(jnp.float32)[None]

    return (shared(feature), shared(hidden))


def solution(mesh):
    sections, dp_count = mesh.shape["section"], mesh.shape["dp"]

    def body(inputs, gain, repeats, order, hidden_grad):
        aligned = (
            inputs.shape[0] == sections == 4
            and inputs.shape[2] * sections % (16 * BLK) == 0
            and inputs.shape[1] % 16 == 0
            and dp_count == 8
            and AWIN == dp_count * 3 * BLK
            and GWIN % (dp_count * 4 * BLK) == 0
        )
        return (fast_body if aligned else plain_body)(inputs, gain, repeats, order, hidden_grad)

    placed = (
        P(None, "dp", "section"),
        P("section", None),
        P("section"),
        P(),
        P("section", None, "dp", None),
    )
    return jax.shard_map(
        body,
        mesh=mesh,
        in_specs=placed,
        out_specs=(P("section", "dp", None), P("section", "dp", None)),
        check_vma=False,
    )
```

profile of v0, /device:TPU:0, one launch (start us, length us, event | category | flops | bytes accessed | tf_op | source)
XLA Modules:
  0.0 53.8 jit_solution(10536107271659690779)
XLA Ops:
  1.3 0.0 copy-start.2
  1.3 1.0 %copy-done.2 = bf16[4,32,1536]{2,1,0:T(8,128)(2,1)S(1)} copy-done((bf16[4,32,1536]{2,1,0:T(8,128)(2,1)S(1)}, bf16[4,32,1536]{2,1,0:T(8,128)(2,1)}, u32[]{:S(2)}) %copy-start.2) | copy-done | bytes 393240
  2.3 0.0 copy-start.4
  2.3 0.7 %copy-done.4 = f32[1,6144]{1,0:T(1,128)S(1)} copy-done((f32[1,6144]{1,0:T(1,128)S(1)}, f32[1,6144]{1,0:T(1,128)}, u32[]{:S(2)}) %copy-start.4) | copy-done | bytes 24600
  3.0 0.0 copy-start
  3.0 0.0 copy-start.1
  3.0 0.8 %shard_map.68 = (bf16[496,128]{1,0:T(8,128)(2,1)}, bf16[496,128]{1,0:T(8,128)(2,1)}, bf16[496,128]{1,0:T(8,128)(2,1)}) custom-call(bf16[4,32,1536]{2,1,0:T(8,128)(2,1)S(1)} %copy-done.2, f32[48,128]{1,0:T(8,128)S(1)} %bitcast.3, s32[1]{0:T(128)S(6)} %copy.7.repeats_ref, s32[1]{0:T(128)} %bitcast.1.me_ref), custom_call_target="tpu_custom_call" | custom-call | flops 8589934592 | bytes 1048576 | tf_op jit(solution)/shard_map/pallas_call | solution.py:182
  3.8 3.0 %collective-permute-start = (bf16[496,128]{1,0:T(8,128)(2,1)}, bf16[496,128]{1,0:T(8,128)(2,1)S(1)}, u32[]{:S(2)}, u32[]{:S(2)}) collective-permute-start(bf16[496,128]{1,0:T(8,128)(2,1)} %get-tuple-element.50), channel_id=1, source_target_pairs={{0,8},{8,0},{16,24},{24,16},{1,9},{9,1},{17,25},{25,17},{2,10},{10... | collective-permute-start | bytes 380936 | tf_op jit(solution)/shard_map/ppermute | solution.py:159
  6.9 2.6 %collective-permute-start.1 = (bf16[496,128]{1,0:T(8,128)(2,1)}, bf16[496,128]{1,0:T(8,128)(2,1)S(1)}, u32[]{:S(2)}, u32[]{:S(2)}) collective-permute-start(bf16[496,128]{1,0:T(8,128)(2,1)} %get-tuple-element.51), channel_id=1, source_target_pairs={{0,16},{8,24},{16,0},{24,8},{1,17},{9,25},{17,1},{25,9},{2,18},{10... | collective-permute-start | bytes 380936 | tf_op jit(solution)/shard_map/ppermute | solution.py:159
  9.4 0.0 collective-permute-start.2
  9.4 0.0 copy-done
  9.4 0.0 copy-done.1
  9.5 2.0 %shard_map.70 = bf16[4,2,400,128]{3,2,1,0:T(8,128)(2,1)S(1)} custom-call(s32[4]{0:T(128)S(1)} %copy-done.1, s32[1]{0:T(128)S(6)} %xor.3._, bf16[1,4,32,12288]{3,2,1,0:T(8,128)(2,1)S(1)} %copy-done, bf16[1,4,32,12288]{3,2,1,0:T(8,128)(2,1)S(1)} %copy-done), custom_call_target="tpu_custom_call" | custom-call | flops 1048576 | bytes 1024 | tf_op jit(solution)/shard_map/pallas_call | solution.py:80
  11.5 0.0 copy-start.3
  11.5 0.0 copy-start.5
  11.5 0.1 collective-permute-start.3
  11.6 2.0 %shard_map.69.near_ref = bf16[4,2,400,128]{3,2,1,0:T(8,128)(2,1)S(1)} custom-call(s32[4]{0:T(128)S(1)} %copy-done.1, s32[1]{0:T(128)} %bitcast.2._, bf16[1,4,32,12288]{3,2,1,0:T(8,128)(2,1)S(1)} %copy-done, bf16[1,4,32,12288]{3,2,1,0:T(8,128)(2,1)S(1)} %copy-done), custom_call_target="tpu_custom_call" | custom-call | flops 17179869184 | bytes 1024 | tf_op jit(solution)/shard_map/pallas_call | solution.py:80
  13.6 0.1 pad_add_fusion.me_ref
  13.6 0.2 collective-permute-done.3.came_ref
  13.9 0.2 shard_map.71
  14.1 0.0 collective-permute-done.refs_0_
  14.1 5.6 %collective-permute-done.1.refs_1_ = bf16[496,128]{1,0:T(8,128)(2,1)S(1)} collective-permute-done((bf16[496,128]{1,0:T(8,128)(2,1)}, bf16[496,128]{1,0:T(8,128)(2,1)S(1)}, u32[]{:S(2)}, u32[]{:S(2)}) %collective-permute-start.1) | collective-permute-done | bytes 127008 | tf_op jit(solution)/shard_map/ppermute | solution.py:159
  19.7 0.0 collective-permute-done.2.refs_2_
  19.7 1.5 %collective-permute-start.4 = (bf16[2,400,128]{2,1,0:T(8,128)(2,1)S(1)}, bf16[2,400,128]{2,1,0:T(8,128)(2,1)S(1)}, u32[]{:S(2)}, u32[]{:S(2)}) collective-permute-start(bf16[2,400,128]{2,1,0:T(8,128)(2,1)S(1)} %get-tuple-element.65), channel_id=1, source_target_pairs={{0,2},{1,3},{2,0},{3,1},{4,6},{5,7},{6,4},{7,5},{8,10},{9,11},{10,... | collective-permute-start | bytes 614408 | tf_op jit(solution)/shard_map/ppermute | solution.py:159
  21.2 1.5 %collective-permute-start.5 = (bf16[2,400,128]{2,1,0:T(8,128)(2,1)S(1)}, bf16[2,400,128]{2,1,0:T(8,128)(2,1)S(1)}, u32[]{:S(2)}, u32[]{:S(2)}) collective-permute-start(bf16[2,400,128]{2,1,0:T(8,128)(2,1)S(1)} %get-tuple-element.66), channel_id=1, source_target_pairs={{0,4},{1,5},{2,6},{3,7},{4,0},{5,1},{6,2},{7,3},{8,12},{9,13},{10,... | collective-permute-start | bytes 614408 | tf_op jit(solution)/shard_map/ppermute | solution.py:159
  22.7 0.0 copy-done.3
  22.7 0.0 copy-done.5
  22.7 7.4 %shard_map.72 = (bf16[4,32,384]{2,1,0:T(8,128)(2,1)S(1)}, bf16[4,32,384]{2,1,0:T(8,128)(2,1)S(1)}, bf16[4,32,384]{2,1,0:T(8,128)(2,1)S(1)}, bf16[4,32,384]{2,1,0...) custom-call(bf16[4,32,1536]{2,1,0:T(8,128)(2,1)S(1)} %copy-done.3, ...), custom_call_target="tpu_custom_call" | custom-call | flops 8589934592 | bytes 2097152 | tf_op jit(solution)/shard_map/pallas_call | solution.py:262
  30.1 0.0 collective-permute-done.4.came_x_ref
  30.1 0.0 collective-permute-done.5.came_y_ref
  30.1 0.5 %collective-permute-start.6 = (bf16[4,32,384]{2,1,0:T(8,128)(2,1)S(1)}, bf16[4,32,384]{2,1,0:T(8,128)(2,1)S(1)}, u32[]{:S(2)}, u32[]{:S(2)}) collective-permute-start(bf16[4,32,384]{2,1,0:T(8,128)(2,1)S(1)} %get-tuple-element.68), channel_id=1, source_target_pairs={{0,6},{1,7},{2,4},{3,5},{4,2},{5,3},{6,0},{7,1},{8,14},{9,15},{10,... | collective-permute-start | bytes 294920 | tf_op jit(solution)/shard_map/ppermute | solution.py:159
  30.7 0.0 collective-permute-start.7
  30.7 1.5 %collective-permute-start.8 = (bf16[4,32,384]{2,1,0:T(8,128)(2,1)S(1)}, bf16[4,32,384]{2,1,0:T(8,128)(2,1)S(1)}, u32[]{:S(2)}, u32[]{:S(2)}) collective-permute-start(bf16[4,32,384]{2,1,0:T(8,128)(2,1)S(1)} %get-tuple-element.70), channel_id=1, source_target_pairs={{0,4},{1,5},{2,6},{3,7},{4,0},{5,1},{6,2},{7,3},{8,12},{9,13},{10,... | collective-permute-start | bytes 294920 | tf_op jit(solution)/shard_map/ppermute | solution.py:159
  32.2 1.5 %collective-permute-start.9 = (bf16[4,32,384]{2,1,0:T(8,128)(2,1)S(1)}, bf16[4,32,384]{2,1,0:T(8,128)(2,1)S(1)}, u32[]{:S(2)}, u32[]{:S(2)}) collective-permute-start(bf16[4,32,384]{2,1,0:T(8,128)(2,1)S(1)} %get-tuple-element.71), channel_id=1, source_target_pairs={{0,2},{1,3},{2,0},{3,1},{4,6},{5,7},{6,4},{7,5},{8,10},{9,11},{10,... | collective-permute-start | bytes 294920 | tf_op jit(solution)/shard_map/ppermute | solution.py:159
  33.7 1.2 %collective-permute-start.10 = (bf16[4,32,384]{2,1,0:T(8,128)(2,1)S(1)}, bf16[4,32,384]{2,1,0:T(8,128)(2,1)S(1)}, u32[]{:S(2)}, u32[]{:S(2)}) collective-permute-start(bf16[4,32,384]{2,1,0:T(8,128)(2,1)S(1)} %get-tuple-element.72), channel_id=1, source_target_pairs={{0,5},{1,4},{2,7},{3,6},{4,1},{5,0},{6,3},{7,2},{8,13},{9,12},{10,... | collective-permute-start | bytes 294920 | tf_op jit(solution)/shard_map/ppermute | solution.py:159
  34.8 1.9 %collective-permute-done.6.refs_1_ = bf16[4,32,384]{2,1,0:T(8,128)(2,1)S(1)} collective-permute-done((bf16[4,32,384]{2,1,0:T(8,128)(2,1)S(1)}, bf16[4,32,384]{2,1,0:T(8,128)(2,1)S(1)}, u32[]{:S(2)}, u32[]{:S(2)}) %collective-permute-start.6) | collective-permute-done | bytes 98336 | tf_op jit(solution)/shard_map/ppermute | solution.py:159
  36.8 0.0 collective-permute-start.11
  36.8 0.0 collective-permute-done.7.refs_2_
  36.8 1.5 %collective-permute-start.12 = (bf16[4,32,384]{2,1,0:T(8,128)(2,1)S(1)}, bf16[4,32,384]{2,1,0:T(8,128)(2,1)S(1)}, u32[]{:S(2)}, u32[]{:S(2)}) collective-permute-start(bf16[4,32,384]{2,1,0:T(8,128)(2,1)S(1)} %get-tuple-element.74), channel_id=1, source_target_pairs={{0,1},{1,0},{2,3},{3,2},{4,5},{5,4},{6,7},{7,6},{8,9},{9,8},{10,11... | collective-permute-start | bytes 294920 | tf_op jit(solution)/shard_map/ppermute | solution.py:159
  38.3 0.7 %collective-permute-done.8.refs_3_ = bf16[4,32,384]{2,1,0:T(8,128)(2,1)S(1)} collective-permute-done((bf16[4,32,384]{2,1,0:T(8,128)(2,1)S(1)}, bf16[4,32,384]{2,1,0:T(8,128)(2,1)S(1)}, u32[]{:S(2)}, u32[]{:S(2)}) %collective-permute-start.8) | collective-permute-done | bytes 98336 | tf_op jit(solution)/shard_map/ppermute | solution.py:159
  39.0 0.0 collective-permute-done.9.refs_4_
  39.0 2.6 %collective-permute-done.10.refs_5_ = bf16[4,32,384]{2,1,0:T(8,128)(2,1)S(1)} collective-permute-done((bf16[4,32,384]{2,1,0:T(8,128)(2,1)S(1)}, bf16[4,32,384]{2,1,0:T(8,128)(2,1)S(1)}, u32[]{:S(2)}, u32[]{:S(2)}) %collective-permute-start.10) | collective-permute-done | bytes 98336 | tf_op jit(solution)/shard_map/ppermute | solution.py:159
  41.6 0.0 collective-permute-done.11.refs_6_
  41.6 0.0 collective-permute-done.12.refs_7_
  41.6 1.0 %shard_map.73 = (f32[208,128]{1,0:T(8,128)S(1)}, bf16[208,128]{1,0:T(8,128)(2,1)S(1)}, bf16[208,128]{1,0:T(8,128)(2,1)S(1)}, bf16[208,128]{1,0:T(8,128)(2,1)S(1)}) custom-call(s32[4]{0:T(128)S(1)} %copy-done.1, s32[1]{0:T(128)} %bitcast.1.me_ref, bf16[4,32,384]{2,1,0:T(8,128)(2,1)S(1)} %get-tuple-element.67.refs_0_, ...), custom_call_target="tpu_custom_call" | custom-call | flops 2147483648 | bytes 1048576 | tf_op jit(solution)/shard_map/pallas_call | solution.py:317
  42.6 3.1 %collective-permute-start.13 = (bf16[208,128]{1,0:T(8,128)(2,1)S(1)}, bf16[208,128]{1,0:T(8,128)(2,1)S(1)}, u32[]{:S(2)}, u32[]{:S(2)}) collective-permute-start(bf16[208,128]{1,0:T(8,128)(2,1)S(1)} %get-tuple-element.83), channel_id=1, source_target_pairs={{0,16},{8,24},{16,0},{24,8},{1,17},{9,25},{17,1},{25,9},{2,18},{10... | collective-permute-start | bytes 159752 | tf_op jit(solution)/shard_map/ppermute | solution.py:159
  45.7 1.3 %collective-permute-start.14 = (bf16[208,128]{1,0:T(8,128)(2,1)S(1)}, bf16[208,128]{1,0:T(8,128)(2,1)S(1)}, u32[]{:S(2)}, u32[]{:S(2)}) collective-permute-start(bf16[208,128]{1,0:T(8,128)(2,1)S(1)} %get-tuple-element.84), channel_id=1, source_target_pairs={{0,24},{8,16},{16,8},{24,0},{1,25},{9,17},{17,9},{25,1},{2,26},{10... | collective-permute-start | bytes 159752 | tf_op jit(solution)/shard_map/ppermute | solution.py:159
  47.0 0.0 collective-permute-start.15
  47.0 0.1 shard_map.74
  47.1 1.0 %collective-permute-start.16 = (bf16[400,128]{1,0:T(8,128)(2,1)S(1)}, bf16[400,128]{1,0:T(8,128)(2,1)S(1)}, u32[]{:S(2)}, u32[]{:S(2)}) collective-permute-start(bf16[400,128]{1,0:T(8,128)(2,1)S(1)} %get-tuple-element.88), channel_id=1, source_target_pairs={{0,4},{1,5},{2,6},{3,7},{4,0},{5,1},{6,2},{7,3},{8,12},{9,13},{10,... | collective-permute-start | bytes 307208 | tf_op jit(solution)/shard_map/ppermute | solution.py:159
  48.1 0.5 collective-permute-start.17
  48.6 0.7 %collective-permute-done.13.refs_1_ = bf16[208,128]{1,0:T(8,128)(2,1)S(1)} collective-permute-done((bf16[208,128]{1,0:T(8,128)(2,1)S(1)}, bf16[208,128]{1,0:T(8,128)(2,1)S(1)}, u32[]{:S(2)}, u32[]{:S(2)}) %collective-permute-start.13) | collective-permute-done | bytes 53280 | tf_op jit(solution)/shard_map/ppermute | solution.py:159
  49.3 2.4 %collective-permute-done.14.refs_2_ = bf16[208,128]{1,0:T(8,128)(2,1)S(1)} collective-permute-done((bf16[208,128]{1,0:T(8,128)(2,1)S(1)}, bf16[208,128]{1,0:T(8,128)(2,1)S(1)}, u32[]{:S(2)}, u32[]{:S(2)}) %collective-permute-start.14) | collective-permute-done | bytes 53280 | tf_op jit(solution)/shard_map/ppermute | solution.py:159
  51.7 0.0 collective-permute-done.15.refs_3_
  51.7 0.8 %shard_map.75 = f32[1,384,128]{2,1,0:T(8,128)} custom-call(f32[208,128]{1,0:T(8,128)S(1)} %get-tuple-element.82.refs_0_, bf16[208,128]{1,0:T(8,128)(2,1)S(1)} %collective-permute-done.13.refs_1_, bf16[208,128]{1,0:T(8,128)(2,1)S(1)} %collective-permute-done.14.refs_2_, bf16[208,128]{1,0:T(8,128)(2,1)S(1)} %collective-permute-done.15.refs_3_), custom_call_target="tpu_custom_call" | custom-call | flops 17179869184 | bytes 1024 | tf_op jit(solution)/shard_map/pallas_call | solution.py:95
  52.5 0.0 collective-permute-done.16.came_y_ref
  52.5 0.2 collective-permute-done.17.came_x_ref
  52.7 1.1 %shard_map.76 = f32[1,1536,128]{2,1,0:T(8,128)} custom-call(f32[2,400,128]{2,1,0:T(8,128)S(1)} %get-tuple-element.87.kept_ref, bf16[400,128]{1,0:T(8,128)(2,1)S(1)} %collective-permute-done.16.came_y_ref, bf16[400,128]{1,0:T(8,128)(2,1)S(1)} %collective-permute-done.17.came_x_ref), custom_call_target="tpu_custom_call" | custom-call | flops 1048576 | bytes 1024 | tf_op jit(solution)/shard_map/pallas_call | solution.py:95
Async XLA Ops:
  1.3 1.0 %copy-start.2 = (bf16[4,32,1536]{2,1,0:T(8,128)(2,1)S(1)}, bf16[4,32,1536]{2,1,0:T(8,128)(2,1)}, u32[]{:S(2)}) copy-start(bf16[4,32,1536]{2,1,0:T(8,128)(2,1)} %own_ref.1) | copy-start | bytes 1179652
  2.3 0.7 %copy-start.4 = (f32[1,6144]{1,0:T(1,128)S(1)}, f32[1,6144]{1,0:T(1,128)}, u32[]{:S(2)}) copy-start(f32[1,6144]{1,0:T(1,128)} %param.6) | copy-start | bytes 73732
  3.0 6.4 %copy-start = (bf16[1,4,32,12288]{3,2,1,0:T(8,128)(2,1)S(1)}, bf16[1,4,32,12288]{3,2,1,0:T(8,128)(2,1)}, u32[]{:S(2)}) copy-start(bf16[1,4,32,12288]{3,2,1,0:T(8,128)(2,1)} %refs_1_.3) | copy-start | bytes 9437188
  3.0 6.4 %copy-start.1 = (s32[4]{0:T(128)S(1)}, s32[4]{0:T(128)}, u32[]{:S(2)}) copy-start(s32[4]{0:T(128)} %order_ref.2) | copy-start | bytes 52
  3.8 10.2 %collective-permute-start = (bf16[496,128]{1,0:T(8,128)(2,1)}, bf16[496,128]{1,0:T(8,128)(2,1)S(1)}, u32[]{:S(2)}, u32[]{:S(2)}) collective-permute-start(bf16[496,128]{1,0:T(8,128)(2,1)} %get-tuple-element.50), channel_id=1, source_target_pairs={{0,8},{8,0},{16,24},{24,16},{1,9},{9,1},{17,25},{25,17},{2,10},{10... | collective-permute-start | bytes 380936 | tf_op jit(solution)/shard_map/ppermute | solution.py:159
  6.9 12.8 %collective-permute-start.1 = (bf16[496,128]{1,0:T(8,128)(2,1)}, bf16[496,128]{1,0:T(8,128)(2,1)S(1)}, u32[]{:S(2)}, u32[]{:S(2)}) collective-permute-start(bf16[496,128]{1,0:T(8,128)(2,1)} %get-tuple-element.51), channel_id=1, source_target_pairs={{0,16},{8,24},{16,0},{24,8},{1,17},{9,25},{17,1},{25,9},{2,18},{10... | collective-permute-start | bytes 380936 | tf_op jit(solution)/shard_map/ppermute | solution.py:159
  9.4 10.2 %collective-permute-start.2 = (bf16[496,128]{1,0:T(8,128)(2,1)}, bf16[496,128]{1,0:T(8,128)(2,1)S(1)}, u32[]{:S(2)}, u32[]{:S(2)}) collective-permute-start(bf16[496,128]{1,0:T(8,128)(2,1)} %get-tuple-element.52), channel_id=1, source_target_pairs={{0,24},{8,16},{16,8},{24,0},{1,25},{9,17},{17,9},{25,1},{2,26},{10... | collective-permute-start | bytes 380936 | tf_op jit(solution)/shard_map/ppermute | solution.py:159
  11.5 11.2 %copy-start.3 = (bf16[4,32,1536]{2,1,0:T(8,128)(2,1)S(1)}, bf16[4,32,1536]{2,1,0:T(8,128)(2,1)}, u32[]{:S(2)}) copy-start(bf16[4,32,1536]{2,1,0:T(8,128)(2,1)} %own_ref.1) | copy-start | bytes 1179652
  11.5 11.2 %copy-start.5 = (f32[1,6144]{1,0:T(1,128)S(1)}, f32[1,6144]{1,0:T(1,128)}, u32[]{:S(2)}) copy-start(f32[1,6144]{1,0:T(1,128)} %param.6) | copy-start | bytes 73732
  11.5 2.4 %collective-permute-start.3 = (bf16[4,2,400,128]{3,2,1,0:T(8,128)(2,1)S(1)}, bf16[4,2,400,128]{3,2,1,0:T(8,128)(2,1)S(1)}, u32[]{:S(2)}, u32[]{:S(2)}) collective-permute-start(bf16[4,2,400,128]{3,2,1,0:T(8,128)(2,1)S(1)} %shard_map.70), channel_id=1, source_target_pairs={{0,1},{1,0},{2,3},{3,2},{4,5},{5,4},{6,7},{7,6},{8,9},{9,8},{10,11... | collective-permute-start | bytes 2457608 | tf_op jit(solution)/shard_map/ppermute | solution.py:159
  19.7 10.4 %collective-permute-start.4 = (bf16[2,400,128]{2,1,0:T(8,128)(2,1)S(1)}, bf16[2,400,128]{2,1,0:T(8,128)(2,1)S(1)}, u32[]{:S(2)}, u32[]{:S(2)}) collective-permute-start(bf16[2,400,128]{2,1,0:T(8,128)(2,1)S(1)} %get-tuple-element.65), channel_id=1, source_target_pairs={{0,2},{1,3},{2,0},{3,1},{4,6},{5,7},{6,4},{7,5},{8,10},{9,11},{10,... | collective-permute-start | bytes 614408 | tf_op jit(solution)/shard_map/ppermute | solution.py:159
  21.2 8.9 %collective-permute-start.5 = (bf16[2,400,128]{2,1,0:T(8,128)(2,1)S(1)}, bf16[2,400,128]{2,1,0:T(8,128)(2,1)S(1)}, u32[]{:S(2)}, u32[]{:S(2)}) collective-permute-start(bf16[2,400,128]{2,1,0:T(8,128)(2,1)S(1)} %get-tuple-element.66), channel_id=1, source_target_pairs={{0,4},{1,5},{2,6},{3,7},{4,0},{5,1},{6,2},{7,3},{8,12},{9,13},{10,... | collective-permute-start | bytes 614408 | tf_op jit(solution)/shard_map/ppermute | solution.py:159
  30.1 6.6 %collective-permute-start.6 = (bf16[4,32,384]{2,1,0:T(8,128)(2,1)S(1)}, bf16[4,32,384]{2,1,0:T(8,128)(2,1)S(1)}, u32[]{:S(2)}, u32[]{:S(2)}) collective-permute-start(bf16[4,32,384]{2,1,0:T(8,128)(2,1)S(1)} %get-tuple-element.68), channel_id=1, source_target_pairs={{0,6},{1,7},{2,4},{3,5},{4,2},{5,3},{6,0},{7,1},{8,14},{9,15},{10,... | collective-permute-start | bytes 294920 | tf_op jit(solution)/shard_map/ppermute | solution.py:159
  30.7 6.1 %collective-permute-start.7 = (bf16[4,32,384]{2,1,0:T(8,128)(2,1)S(1)}, bf16[4,32,384]{2,1,0:T(8,128)(2,1)S(1)}, u32[]{:S(2)}, u32[]{:S(2)}) collective-permute-start(bf16[4,32,384]{2,1,0:T(8,128)(2,1)S(1)} %get-tuple-element.69), channel_id=1, source_target_pairs={{0,7},{1,6},{2,5},{3,4},{4,3},{5,2},{6,1},{7,0},{8,15},{9,14},{10,... | collective-permute-start | bytes 294920 | tf_op jit(solution)/shard_map/ppermute | solution.py:159
  30.7 8.3 %collective-permute-start.8 = (bf16[4,32,384]{2,1,0:T(8,128)(2,1)S(1)}, bf16[4,32,384]{2,1,0:T(8,128)(2,1)S(1)}, u32[]{:S(2)}, u32[]{:S(2)}) collective-permute-start(bf16[4,32,384]{2,1,0:T(8,128)(2,1)S(1)} %get-tuple-element.70), channel_id=1, source_target_pairs={{0,4},{1,5},{2,6},{3,7},{4,0},{5,1},{6,2},{7,3},{8,12},{9,13},{10,... | collective-permute-start | bytes 294920 | tf_op jit(solution)/shard_map/ppermute | solution.py:159
  32.2 6.8 %collective-permute-start.9 = (bf16[4,32,384]{2,1,0:T(8,128)(2,1)S(1)}, bf16[4,32,384]{2,1,0:T(8,128)(2,1)S(1)}, u32[]{:S(2)}, u32[]{:S(2)}) collective-permute-start(bf16[4,32,384]{2,1,0:T(8,128)(2,1)S(1)} %get-tuple-element.71), channel_id=1, source_target_pairs={{0,2},{1,3},{2,0},{3,1},{4,6},{5,7},{6,4},{7,5},{8,10},{9,11},{10,... | collective-permute-start | bytes 294920 | tf_op jit(solution)/shard_map/ppermute | solution.py:159
  33.7 7.9 %collective-permute-start.10 = (bf16[4,32,384]{2,1,0:T(8,128)(2,1)S(1)}, bf16[4,32,384]{2,1,0:T(8,128)(2,1)S(1)}, u32[]{:S(2)}, u32[]{:S(2)}) collective-permute-start(bf16[4,32,384]{2,1,0:T(8,128)(2,1)S(1)} %get-tuple-element.72), channel_id=1, source_target_pairs={{0,5},{1,4},{2,7},{3,6},{4,1},{5,0},{6,3},{7,2},{8,13},{9,12},{10,... | collective-permute-start | bytes 294920 | tf_op jit(solution)/shard_map/ppermute | solution.py:159
  36.8 4.8 %collective-permute-start.11 = (bf16[4,32,384]{2,1,0:T(8,128)(2,1)S(1)}, bf16[4,32,384]{2,1,0:T(8,128)(2,1)S(1)}, u32[]{:S(2)}, u32[]{:S(2)}) collective-permute-start(bf16[4,32,384]{2,1,0:T(8,128)(2,1)S(1)} %get-tuple-element.73), channel_id=1, source_target_pairs={{0,3},{1,2},{2,1},{3,0},{4,7},{5,6},{6,5},{7,4},{8,11},{9,10},{10,... | collective-permute-start | bytes 294920 | tf_op jit(solution)/shard_map/ppermute | solution.py:159
  36.8 4.8 %collective-permute-start.12 = (bf16[4,32,384]{2,1,0:T(8,128)(2,1)S(1)}, bf16[4,32,384]{2,1,0:T(8,128)(2,1)S(1)}, u32[]{:S(2)}, u32[]{:S(2)}) collective-permute-start(bf16[4,32,384]{2,1,0:T(8,128)(2,1)S(1)} %get-tuple-element.74), channel_id=1, source_target_pairs={{0,1},{1,0},{2,3},{3,2},{4,5},{5,4},{6,7},{7,6},{8,9},{9,8},{10,11... | collective-permute-start | bytes 294920 | tf_op jit(solution)/shard_map/ppermute | solution.py:159
  42.6 6.7 %collective-permute-start.13 = (bf16[208,128]{1,0:T(8,128)(2,1)S(1)}, bf16[208,128]{1,0:T(8,128)(2,1)S(1)}, u32[]{:S(2)}, u32[]{:S(2)}) collective-permute-start(bf16[208,128]{1,0:T(8,128)(2,1)S(1)} %get-tuple-element.83), channel_id=1, source_target_pairs={{0,16},{8,24},{16,0},{24,8},{1,17},{9,25},{17,1},{25,9},{2,18},{10... | collective-permute-start | bytes 159752 | tf_op jit(solution)/shard_map/ppermute | solution.py:159
  45.7 6.0 %collective-permute-start.14 = (bf16[208,128]{1,0:T(8,128)(2,1)S(1)}, bf16[208,128]{1,0:T(8,128)(2,1)S(1)}, u32[]{:S(2)}, u32[]{:S(2)}) collective-permute-start(bf16[208,128]{1,0:T(8,128)(2,1)S(1)} %get-tuple-element.84), channel_id=1, source_target_pairs={{0,24},{8,16},{16,8},{24,0},{1,25},{9,17},{17,9},{25,1},{2,26},{10... | collective-permute-start | bytes 159752 | tf_op jit(solution)/shard_map/ppermute | solution.py:159
  47.0 4.7 %collective-permute-start.15 = (bf16[208,128]{1,0:T(8,128)(2,1)S(1)}, bf16[208,128]{1,0:T(8,128)(2,1)S(1)}, u32[]{:S(2)}, u32[]{:S(2)}) collective-permute-start(bf16[208,128]{1,0:T(8,128)(2,1)S(1)} %get-tuple-element.85), channel_id=1, source_target_pairs={{0,8},{8,0},{16,24},{24,16},{1,9},{9,1},{17,25},{25,17},{2,10},{10... | collective-permute-start | bytes 159752 | tf_op jit(solution)/shard_map/ppermute | solution.py:159
  47.1 5.5 %collective-permute-start.16 = (bf16[400,128]{1,0:T(8,128)(2,1)S(1)}, bf16[400,128]{1,0:T(8,128)(2,1)S(1)}, u32[]{:S(2)}, u32[]{:S(2)}) collective-permute-start(bf16[400,128]{1,0:T(8,128)(2,1)S(1)} %get-tuple-element.88), channel_id=1, source_target_pairs={{0,4},{1,5},{2,6},{3,7},{4,0},{5,1},{6,2},{7,3},{8,12},{9,13},{10,... | collective-permute-start | bytes 307208 | tf_op jit(solution)/shard_map/ppermute | solution.py:159
  48.1 4.7 %collective-permute-start.17 = (bf16[400,128]{1,0:T(8,128)(2,1)S(1)}, bf16[400,128]{1,0:T(8,128)(2,1)S(1)}, u32[]{:S(2)}, u32[]{:S(2)}) collective-permute-start(bf16[400,128]{1,0:T(8,128)(2,1)S(1)} %get-tuple-element.89), channel_id=1, source_target_pairs={{0,2},{1,3},{2,0},{3,1},{4,6},{5,7},{6,4},{7,5},{8,10},{9,11},{10,... | collective-permute-start | bytes 307208 | tf_op jit(solution)/shard_map/ppermute | solution.py:159
where the time goes:
time: 54.3 us; the launch traced here: 53.8 us
  starting transfers between devices  20.8 us (38%)
  Pallas kernels  15.4 us (28%)
  waiting for transfers between devices  14.4 us (27%)
  local copies, waits for them, and re-layouts  1.75 us (3%)
  between operations  1.4 us (3%)
    ppermute x18, starting transfers between devices, swapped(): lax.ppermute(shard, axis, [(i, i ^ mask) for i in range(lax.axis_size(axi...  20.8 us
    ppermute x18, waiting for transfers between devices, swapped(): lax.ppermute(shard, axis, [(i, i ^ mask) for i in range(lax.axis_size(axi...  14.4 us
    pallas_call x1, Pallas kernels, relay(): pl.pallas_call(functools.partial(relay_kernel, sections, owners), out_sha...  7.4 us
    pallas_call x2, Pallas kernels, hidden_terms(): pl.pallas_call(functools.partial(hidden_kernel, micro, pairs, scale), out...  4 us
    pallas_call x4, Pallas kernels, small_call(): pl.pallas_call(kernel, out_shape=shapes, in_specs=[VMEM_SPEC] * len(opera...  2.16 us
    unnamed x12, local copies, waits for them, and re-layouts  1.75 us
  transfers between devices with their start and end apart: 18, of which 8 were waited for; matrix products, arithmetic and copies ran while one was open for 0% of the time, Pallas kernels for 23%

commit v1 on v0

--- a/solution.py
+++ b/solution.py
@@ -184,7 +184,7 @@
         out_shape=(shape,) * (micro - 1),
         in_specs=[VMEM_SPEC, VMEM_SPEC, SMEM_SPEC, SMEM_SPEC],
         out_specs=(VMEM_SPEC,) * (micro - 1),
-        compiler_params=params(),
+        compiler_params=params(60 * 1024 * 1024),
         cost_estimate=pl.CostEstimate(flops=1 << 33, bytes_accessed=1 << 20, transcendentals=0),
     )(inputs, gain, repeats, me)
 
@@ -266,7 +266,7 @@
         out_specs=(VMEM_SPEC,) * owners,
         scratch_shapes=[pltpu.VMEM((chunks, rows, BLK), jnp.float32), pltpu.VMEM((sections, chunks + 8, BLK), jnp.float32)],
         compiler_params=params(),
-        cost_estimate=pl.CostEstimate(flops=1 << 33, bytes_accessed=2 << 20, transcendentals=0),
+        cost_estimate=pl.CostEstimate(flops=1 << 31, bytes_accessed=2 << 20, transcendentals=0),
     )(inputs, gain, repeats, me, *received)
 
 

time: 54.3 us -> 51.6 us (0.950)
  waiting for transfers between devices: 14.4 us -> 10.6 us
  starting transfers between devices: 20.8 us -> 22.6 us
  local copies, waits for them, and re-layouts: 1.75 us -> 0.02 us
  Pallas kernels: 15.4 us -> 16.5 us
    ppermute x18, waiting for transfers between devices: 14.4 us -> 10.6 us  [swapped(): lax.ppermute(shard, axis, [(i, i ^ mask) for i in range(lax.axis_size(axi...]
    ppermute x18, starting transfers between devices: 20.8 us -> 22.6 us  [swapped(): lax.ppermute(shard, axis, [(i, i ^ mask) for i in range(lax.axis_size(axi...]
    unnamed x12 -> x8, local copies, waits for them, and re-layouts: 1.75 us -> 0.02 us
    pallas_call x1, Pallas kernels: 0.8 us -> 1.94 us  [messages(): pl.pallas_call(message_kernel, out_shape=(shape,) * (micro - 1), in_specs...]
  transfers between devices with their start and end apart: 18 -> 18, of which waited for: 8 -> 8; matrix products, arithmetic and copies ran while one was open for 0% -> 0% of each run, Pallas kernels for 23% -> 24%
where the time goes in v1:
time: 51.6 us; the launch traced here: 51.2 us
  starting transfers between devices  22.6 us (44%)
  Pallas kernels  16.5 us (32%)
  waiting for transfers between devices  10.6 us (21%)
  between operations  1.4 us (3%)
    ppermute x18, starting transfers between devices, swapped(): lax.ppermute(shard, axis, [(i, i ^ mask) for i in range(lax.axis_size(axi...  22.6 us
    ppermute x18, waiting for transfers between devices, swapped(): lax.ppermute(shard, axis, [(i, i ^ mask) for i in range(lax.axis_size(axi...  10.6 us
    pallas_call x1, Pallas kernels, relay(): pl.pallas_call(functools.partial(relay_kernel, sections, owners), out_sha...  7.4 us
    pallas_call x2, Pallas kernels, hidden_terms(): pl.pallas_call(functools.partial(hidden_kernel, micro, pairs, scale), out...  4 us
    pallas_call x4, Pallas kernels, small_call(): pl.pallas_call(kernel, out_shape=shapes, in_specs=[VMEM_SPEC] * len(opera...  2.16 us
    pallas_call x1, Pallas kernels, messages(): pl.pallas_call(message_kernel, out_shape=(shape,) * (micro - 1), in_specs...  1.94 us
  transfers between devices with their start and end apart: 18, of which 8 were waited for; matrix products, arithmetic and copies ran while one was open for 0% of the time, Pallas kernels for 24%

profile of v1, /device:TPU:0, one launch (start us, length us, event | category | flops | bytes accessed | tf_op | source)
XLA Modules:
  0.0 51.2 jit_solution(13437519492276835842)
XLA Ops:
  1.3 0.0 copy-start
  1.3 0.0 copy-start.1
  1.3 1.9 %shard_map.68 = (bf16[496,128]{1,0:T(8,128)(2,1)}, bf16[496,128]{1,0:T(8,128)(2,1)}, bf16[496,128]{1,0:T(8,128)(2,1)}) custom-call(bf16[4,32,1536]{2,1,0:T(8,128)(2,1)} %own_ref.1, f32[48,128]{1,0:T(8,128)} %bitcast.3, s32[1]{0:T(128)S(6)} %copy.7.repeats_ref, s32[1]{0:T(128)} %bitcast.1.me_ref), custom_call_target="tpu_custom_call" | custom-call | flops 8589934592 | bytes 1048576 | tf_op jit(solution)/shard_map/pallas_call | solution.py:182
  3.2 3.0 %collective-permute-start = (bf16[496,128]{1,0:T(8,128)(2,1)}, bf16[496,128]{1,0:T(8,128)(2,1)S(1)}, u32[]{:S(2)}, u32[]{:S(2)}) collective-permute-start(bf16[496,128]{1,0:T(8,128)(2,1)} %get-tuple-element.50), channel_id=1, source_target_pairs={{0,8},{8,0},{16,24},{24,16},{1,9},{9,1},{17,25},{25,17},{2,10},{10... | collective-permute-start | bytes 380936 | tf_op jit(solution)/shard_map/ppermute | solution.py:159
  6.3 2.6 %collective-permute-start.1 = (bf16[496,128]{1,0:T(8,128)(2,1)}, bf16[496,128]{1,0:T(8,128)(2,1)S(1)}, u32[]{:S(2)}, u32[]{:S(2)}) collective-permute-start(bf16[496,128]{1,0:T(8,128)(2,1)} %get-tuple-element.51), channel_id=1, source_target_pairs={{0,16},{8,24},{16,0},{24,8},{1,17},{9,25},{17,1},{25,9},{2,18},{10... | collective-permute-start | bytes 380936 | tf_op jit(solution)/shard_map/ppermute | solution.py:159
  8.9 0.0 collective-permute-start.2
  8.9 0.0 copy-done
  8.9 0.0 copy-done.1
  8.9 2.0 %shard_map.70 = bf16[4,2,400,128]{3,2,1,0:T(8,128)(2,1)S(1)} custom-call(s32[4]{0:T(128)S(1)} %copy-done.1, s32[1]{0:T(128)S(6)} %xor.3._, bf16[1,4,32,12288]{3,2,1,0:T(8,128)(2,1)S(1)} %copy-done, bf16[1,4,32,12288]{3,2,1,0:T(8,128)(2,1)S(1)} %copy-done), custom_call_target="tpu_custom_call" | custom-call | flops 1048576 | bytes 1024 | tf_op jit(solution)/shard_map/pallas_call | solution.py:80
  10.9 0.0 copy-start.2
  10.9 0.0 copy-start.3
  10.9 0.1 collective-permute-start.3
  11.0 2.0 %shard_map.69.near_ref = bf16[4,2,400,128]{3,2,1,0:T(8,128)(2,1)S(1)} custom-call(s32[4]{0:T(128)S(1)} %copy-done.1, s32[1]{0:T(128)} %bitcast.2._, bf16[1,4,32,12288]{3,2,1,0:T(8,128)(2,1)S(1)} %copy-done, bf16[1,4,32,12288]{3,2,1,0:T(8,128)(2,1)S(1)} %copy-done), custom_call_target="tpu_custom_call" | custom-call | flops 17179869184 | bytes 1024 | tf_op jit(solution)/shard_map/pallas_call | solution.py:80
  13.0 0.3 collective-permute-done.3.came_ref
  13.3 0.2 shard_map.71
  13.5 1.8 %collective-permute-start.4 = (bf16[2,400,128]{2,1,0:T(8,128)(2,1)S(1)}, bf16[2,400,128]{2,1,0:T(8,128)(2,1)S(1)}, u32[]{:S(2)}, u32[]{:S(2)}) collective-permute-start(bf16[2,400,128]{2,1,0:T(8,128)(2,1)S(1)} %get-tuple-element.65), channel_id=1, source_target_pairs={{0,2},{1,3},{2,0},{3,1},{4,6},{5,7},{6,4},{7,5},{8,10},{9,11},{10,... | collective-permute-start | bytes 614408 | tf_op jit(solution)/shard_map/ppermute | solution.py:159
  15.2 1.5 %collective-permute-start.5 = (bf16[2,400,128]{2,1,0:T(8,128)(2,1)S(1)}, bf16[2,400,128]{2,1,0:T(8,128)(2,1)S(1)}, u32[]{:S(2)}, u32[]{:S(2)}) collective-permute-start(bf16[2,400,128]{2,1,0:T(8,128)(2,1)S(1)} %get-tuple-element.66), channel_id=1, source_target_pairs={{0,4},{1,5},{2,6},{3,7},{4,0},{5,1},{6,2},{7,3},{8,12},{9,13},{10,... | collective-permute-start | bytes 614408 | tf_op jit(solution)/shard_map/ppermute | solution.py:159
  16.8 0.1 pad_add_fusion.me_ref
  16.8 0.0 collective-permute-done.refs_0_
  16.8 2.2 %collective-permute-done.1.refs_1_ = bf16[496,128]{1,0:T(8,128)(2,1)S(1)} collective-permute-done((bf16[496,128]{1,0:T(8,128)(2,1)}, bf16[496,128]{1,0:T(8,128)(2,1)S(1)}, u32[]{:S(2)}, u32[]{:S(2)}) %collective-permute-start.1) | collective-permute-done | bytes 127008 | tf_op jit(solution)/shard_map/ppermute | solution.py:159
  19.1 0.0 collective-permute-done.2.refs_2_
  19.1 0.0 copy-done.2
  19.1 0.0 copy-done.3
  19.1 7.4 %shard_map.72 = (bf16[4,32,384]{2,1,0:T(8,128)(2,1)S(1)}, bf16[4,32,384]{2,1,0:T(8,128)(2,1)S(1)}, bf16[4,32,384]{2,1,0:T(8,128)(2,1)S(1)}, bf16[4,32,384]{2,1,0...) custom-call(bf16[4,32,1536]{2,1,0:T(8,128)(2,1)S(1)} %copy-done.2, ...), custom_call_target="tpu_custom_call" | custom-call | flops 2147483648 | bytes 2097152 | tf_op jit(solution)/shard_map/pallas_call | solution.py:262
  26.5 0.0 collective-permute-done.4.came_x_ref
  26.5 0.0 collective-permute-done.5.came_y_ref
  26.5 2.5 %collective-permute-start.6 = (bf16[4,32,384]{2,1,0:T(8,128)(2,1)S(1)}, bf16[4,32,384]{2,1,0:T(8,128)(2,1)S(1)}, u32[]{:S(2)}, u32[]{:S(2)}) collective-permute-start(bf16[4,32,384]{2,1,0:T(8,128)(2,1)S(1)} %get-tuple-element.68), channel_id=1, source_target_pairs={{0,6},{1,7},{2,4},{3,5},{4,2},{5,3},{6,0},{7,1},{8,14},{9,15},{10,... | collective-permute-start | bytes 294920 | tf_op jit(solution)/shard_map/ppermute | solution.py:159
  29.1 0.0 collective-permute-start.7
  29.1 0.5 collective-permute-start.8
  29.6 0.5 %collective-permute-start.9 = (bf16[4,32,384]{2,1,0:T(8,128)(2,1)S(1)}, bf16[4,32,384]{2,1,0:T(8,128)(2,1)S(1)}, u32[]{:S(2)}, u32[]{:S(2)}) collective-permute-start(bf16[4,32,384]{2,1,0:T(8,128)(2,1)S(1)} %get-tuple-element.71), channel_id=1, source_target_pairs={{0,2},{1,3},{2,0},{3,1},{4,6},{5,7},{6,4},{7,5},{8,10},{9,11},{10,... | collective-permute-start | bytes 294920 | tf_op jit(solution)/shard_map/ppermute | solution.py:159
  30.1 2.1 %collective-permute-start.10 = (bf16[4,32,384]{2,1,0:T(8,128)(2,1)S(1)}, bf16[4,32,384]{2,1,0:T(8,128)(2,1)S(1)}, u32[]{:S(2)}, u32[]{:S(2)}) collective-permute-start(bf16[4,32,384]{2,1,0:T(8,128)(2,1)S(1)} %get-tuple-element.72), channel_id=1, source_target_pairs={{0,5},{1,4},{2,7},{3,6},{4,1},{5,0},{6,3},{7,2},{8,13},{9,12},{10,... | collective-permute-start | bytes 294920 | tf_op jit(solution)/shard_map/ppermute | solution.py:159
  32.2 0.0 collective-permute-done.6.refs_1_
  32.2 0.6 %collective-permute-start.11 = (bf16[4,32,384]{2,1,0:T(8,128)(2,1)S(1)}, bf16[4,32,384]{2,1,0:T(8,128)(2,1)S(1)}, u32[]{:S(2)}, u32[]{:S(2)}) collective-permute-start(bf16[4,32,384]{2,1,0:T(8,128)(2,1)S(1)} %get-tuple-element.73), channel_id=1, source_target_pairs={{0,3},{1,2},{2,1},{3,0},{4,7},{5,6},{6,5},{7,4},{8,11},{9,10},{10,... | collective-permute-start | bytes 294920 | tf_op jit(solution)/shard_map/ppermute | solution.py:159
  32.8 1.6 %collective-permute-done.7.refs_2_ = bf16[4,32,384]{2,1,0:T(8,128)(2,1)S(1)} collective-permute-done((bf16[4,32,384]{2,1,0:T(8,128)(2,1)S(1)}, bf16[4,32,384]{2,1,0:T(8,128)(2,1)S(1)}, u32[]{:S(2)}, u32[]{:S(2)}) %collective-permute-start.7) | collective-permute-done | bytes 98336 | tf_op jit(solution)/shard_map/ppermute | solution.py:159
  34.4 0.0 collective-permute-start.12
  34.4 1.9 %collective-permute-done.8.refs_3_ = bf16[4,32,384]{2,1,0:T(8,128)(2,1)S(1)} collective-permute-done((bf16[4,32,384]{2,1,0:T(8,128)(2,1)S(1)}, bf16[4,32,384]{2,1,0:T(8,128)(2,1)S(1)}, u32[]{:S(2)}, u32[]{:S(2)}) %collective-permute-start.8) | collective-permute-done | bytes 98336 | tf_op jit(solution)/shard_map/ppermute | solution.py:159
  36.4 0.3 collective-permute-done.9.refs_4_
  36.6 1.8 %collective-permute-done.10.refs_5_ = bf16[4,32,384]{2,1,0:T(8,128)(2,1)S(1)} collective-permute-done((bf16[4,32,384]{2,1,0:T(8,128)(2,1)S(1)}, bf16[4,32,384]{2,1,0:T(8,128)(2,1)S(1)}, u32[]{:S(2)}, u32[]{:S(2)}) %collective-permute-start.10) | collective-permute-done | bytes 98336 | tf_op jit(solution)/shard_map/ppermute | solution.py:159
  38.4 0.0 collective-permute-done.11.refs_6_
  38.4 0.0 collective-permute-done.12.refs_7_
  38.4 1.0 %shard_map.73 = (f32[208,128]{1,0:T(8,128)S(1)}, bf16[208,128]{1,0:T(8,128)(2,1)S(1)}, bf16[208,128]{1,0:T(8,128)(2,1)S(1)}, bf16[208,128]{1,0:T(8,128)(2,1)S(1)}) custom-call(s32[4]{0:T(128)S(1)} %copy-done.1, s32[1]{0:T(128)} %bitcast.1.me_ref, bf16[4,32,384]{2,1,0:T(8,128)(2,1)S(1)} %get-tuple-element.67.refs_0_, ...), custom_call_target="tpu_custom_call" | custom-call | flops 2147483648 | bytes 1048576 | tf_op jit(solution)/shard_map/pallas_call | solution.py:317
  39.4 3.0 %collective-permute-start.13 = (bf16[208,128]{1,0:T(8,128)(2,1)S(1)}, bf16[208,128]{1,0:T(8,128)(2,1)S(1)}, u32[]{:S(2)}, u32[]{:S(2)}) collective-permute-start(bf16[208,128]{1,0:T(8,128)(2,1)S(1)} %get-tuple-element.83), channel_id=1, source_target_pairs={{0,16},{8,24},{16,0},{24,8},{1,17},{9,25},{17,1},{25,9},{2,18},{10... | collective-permute-start | bytes 159752 | tf_op jit(solution)/shard_map/ppermute | solution.py:159
  42.4 1.3 %collective-permute-start.14 = (bf16[208,128]{1,0:T(8,128)(2,1)S(1)}, bf16[208,128]{1,0:T(8,128)(2,1)S(1)}, u32[]{:S(2)}, u32[]{:S(2)}) collective-permute-start(bf16[208,128]{1,0:T(8,128)(2,1)S(1)} %get-tuple-element.84), channel_id=1, source_target_pairs={{0,24},{8,16},{16,8},{24,0},{1,25},{9,17},{17,9},{25,1},{2,26},{10... | collective-permute-start | bytes 159752 | tf_op jit(solution)/shard_map/ppermute | solution.py:159
  43.8 0.0 collective-permute-start.15
  43.8 0.1 shard_map.74
  43.9 1.6 %collective-permute-start.16 = (bf16[400,128]{1,0:T(8,128)(2,1)S(1)}, bf16[400,128]{1,0:T(8,128)(2,1)S(1)}, u32[]{:S(2)}, u32[]{:S(2)}) collective-permute-start(bf16[400,128]{1,0:T(8,128)(2,1)S(1)} %get-tuple-element.88), channel_id=1, source_target_pairs={{0,4},{1,5},{2,6},{3,7},{4,0},{5,1},{6,2},{7,3},{8,12},{9,13},{10,... | collective-permute-start | bytes 307208 | tf_op jit(solution)/shard_map/ppermute | solution.py:159
  45.5 1.4 %collective-permute-start.17 = (bf16[400,128]{1,0:T(8,128)(2,1)S(1)}, bf16[400,128]{1,0:T(8,128)(2,1)S(1)}, u32[]{:S(2)}, u32[]{:S(2)}) collective-permute-start(bf16[400,128]{1,0:T(8,128)(2,1)S(1)} %get-tuple-element.89), channel_id=1, source_target_pairs={{0,2},{1,3},{2,0},{3,1},{4,6},{5,7},{6,4},{7,5},{8,10},{9,11},{10,... | collective-permute-start | bytes 307208 | tf_op jit(solution)/shard_map/ppermute | solution.py:159
  46.9 0.0 collective-permute-done.13.refs_1_
  46.9 1.6 %collective-permute-done.14.refs_2_ = bf16[208,128]{1,0:T(8,128)(2,1)S(1)} collective-permute-done((bf16[208,128]{1,0:T(8,128)(2,1)S(1)}, bf16[208,128]{1,0:T(8,128)(2,1)S(1)}, u32[]{:S(2)}, u32[]{:S(2)}) %collective-permute-start.14) | collective-permute-done | bytes 53280 | tf_op jit(solution)/shard_map/ppermute | solution.py:159
  48.5 0.0 collective-permute-done.15.refs_3_
  48.5 0.8 %shard_map.75 = f32[1,384,128]{2,1,0:T(8,128)} custom-call(f32[208,128]{1,0:T(8,128)S(1)} %get-tuple-element.82.refs_0_, bf16[208,128]{1,0:T(8,128)(2,1)S(1)} %collective-permute-done.13.refs_1_, bf16[208,128]{1,0:T(8,128)(2,1)S(1)} %collective-permute-done.14.refs_2_, bf16[208,128]{1,0:T(8,128)(2,1)S(1)} %collective-permute-done.15.refs_3_), custom_call_target="tpu_custom_call" | custom-call | flops 17179869184 | bytes 1024 | tf_op jit(solution)/shard_map/pallas_call | solution.py:95
  49.3 0.0 collective-permute-done.16.came_y_ref
  49.3 0.8 %collective-permute-done.17.came_x_ref = bf16[400,128]{1,0:T(8,128)(2,1)S(1)} collective-permute-done((bf16[400,128]{1,0:T(8,128)(2,1)S(1)}, bf16[400,128]{1,0:T(8,128)(2,1)S(1)}, u32[]{:S(2)}, u32[]{:S(2)}) %collective-permute-start.17) | collective-permute-done | bytes 102432 | tf_op jit(solution)/shard_map/ppermute | solution.py:159
  50.1 1.1 %shard_map.76 = f32[1,1536,128]{2,1,0:T(8,128)} custom-call(f32[2,400,128]{2,1,0:T(8,128)S(1)} %get-tuple-element.87.kept_ref, bf16[400,128]{1,0:T(8,128)(2,1)S(1)} %collective-permute-done.16.came_y_ref, bf16[400,128]{1,0:T(8,128)(2,1)S(1)} %collective-permute-done.17.came_x_ref), custom_call_target="tpu_custom_call" | custom-call | flops 1048576 | bytes 1024 | tf_op jit(solution)/shard_map/pallas_call | solution.py:95
Async XLA Ops:
  1.3 7.6 %copy-start = (bf16[1,4,32,12288]{3,2,1,0:T(8,128)(2,1)S(1)}, bf16[1,4,32,12288]{3,2,1,0:T(8,128)(2,1)}, u32[]{:S(2)}) copy-start(bf16[1,4,32,12288]{3,2,1,0:T(8,128)(2,1)} %refs_1_.3) | copy-start | bytes 9437188
  1.3 7.6 %copy-start.1 = (s32[4]{0:T(128)S(1)}, s32[4]{0:T(128)}, u32[]{:S(2)}) copy-start(s32[4]{0:T(128)} %order_ref.2) | copy-start | bytes 52
  3.2 13.6 %collective-permute-start = (bf16[496,128]{1,0:T(8,128)(2,1)}, bf16[496,128]{1,0:T(8,128)(2,1)S(1)}, u32[]{:S(2)}, u32[]{:S(2)}) collective-permute-start(bf16[496,128]{1,0:T(8,128)(2,1)} %get-tuple-element.50), channel_id=1, source_target_pairs={{0,8},{8,0},{16,24},{24,16},{1,9},{9,1},{17,25},{25,17},{2,10},{10... | collective-permute-start | bytes 380936 | tf_op jit(solution)/shard_map/ppermute | solution.py:159
  6.3 12.8 %collective-permute-start.1 = (bf16[496,128]{1,0:T(8,128)(2,1)}, bf16[496,128]{1,0:T(8,128)(2,1)S(1)}, u32[]{:S(2)}, u32[]{:S(2)}) collective-permute-start(bf16[496,128]{1,0:T(8,128)(2,1)} %get-tuple-element.51), channel_id=1, source_target_pairs={{0,16},{8,24},{16,0},{24,8},{1,17},{9,25},{17,1},{25,9},{2,18},{10... | collective-permute-start | bytes 380936 | tf_op jit(solution)/shard_map/ppermute | solution.py:159
  8.9 10.2 %collective-permute-start.2 = (bf16[496,128]{1,0:T(8,128)(2,1)}, bf16[496,128]{1,0:T(8,128)(2,1)S(1)}, u32[]{:S(2)}, u32[]{:S(2)}) collective-permute-start(bf16[496,128]{1,0:T(8,128)(2,1)} %get-tuple-element.52), channel_id=1, source_target_pairs={{0,24},{8,16},{16,8},{24,0},{1,25},{9,17},{17,9},{25,1},{2,26},{10... | collective-permute-start | bytes 380936 | tf_op jit(solution)/shard_map/ppermute | solution.py:159
  10.9 8.2 %copy-start.2 = (bf16[4,32,1536]{2,1,0:T(8,128)(2,1)S(1)}, bf16[4,32,1536]{2,1,0:T(8,128)(2,1)}, u32[]{:S(2)}) copy-start(bf16[4,32,1536]{2,1,0:T(8,128)(2,1)} %own_ref.1) | copy-start | bytes 1179652
  10.9 8.2 %copy-start.3 = (f32[1,6144]{1,0:T(1,128)S(1)}, f32[1,6144]{1,0:T(1,128)}, u32[]{:S(2)}) copy-start(f32[1,6144]{1,0:T(1,128)} %param.6) | copy-start | bytes 73732
  10.9 2.4 %collective-permute-start.3 = (bf16[4,2,400,128]{3,2,1,0:T(8,128)(2,1)S(1)}, bf16[4,2,400,128]{3,2,1,0:T(8,128)(2,1)S(1)}, u32[]{:S(2)}, u32[]{:S(2)}) collective-permute-start(bf16[4,2,400,128]{3,2,1,0:T(8,128)(2,1)S(1)} %shard_map.70), channel_id=1, source_target_pairs={{0,1},{1,0},{2,3},{3,2},{4,5},{5,4},{6,7},{7,6},{8,9},{9,8},{10,11... | collective-permute-start | bytes 2457608 | tf_op jit(solution)/shard_map/ppermute | solution.py:159
  13.5 13.0 %collective-permute-start.4 = (bf16[2,400,128]{2,1,0:T(8,128)(2,1)S(1)}, bf16[2,400,128]{2,1,0:T(8,128)(2,1)S(1)}, u32[]{:S(2)}, u32[]{:S(2)}) collective-permute-start(bf16[2,400,128]{2,1,0:T(8,128)(2,1)S(1)} %get-tuple-element.65), channel_id=1, source_target_pairs={{0,2},{1,3},{2,0},{3,1},{4,6},{5,7},{6,4},{7,5},{8,10},{9,11},{10,... | collective-permute-start | bytes 614408 | tf_op jit(solution)/shard_map/ppermute | solution.py:159
  15.2 11.3 %collective-permute-start.5 = (bf16[2,400,128]{2,1,0:T(8,128)(2,1)S(1)}, bf16[2,400,128]{2,1,0:T(8,128)(2,1)S(1)}, u32[]{:S(2)}, u32[]{:S(2)}) collective-permute-start(bf16[2,400,128]{2,1,0:T(8,128)(2,1)S(1)} %get-tuple-element.66), channel_id=1, source_target_pairs={{0,4},{1,5},{2,6},{3,7},{4,0},{5,1},{6,2},{7,3},{8,12},{9,13},{10,... | collective-permute-start | bytes 614408 | tf_op jit(solution)/shard_map/ppermute | solution.py:159
  26.5 5.7 %collective-permute-start.6 = (bf16[4,32,384]{2,1,0:T(8,128)(2,1)S(1)}, bf16[4,32,384]{2,1,0:T(8,128)(2,1)S(1)}, u32[]{:S(2)}, u32[]{:S(2)}) collective-permute-start(bf16[4,32,384]{2,1,0:T(8,128)(2,1)S(1)} %get-tuple-element.68), channel_id=1, source_target_pairs={{0,6},{1,7},{2,4},{3,5},{4,2},{5,3},{6,0},{7,1},{8,14},{9,15},{10,... | collective-permute-start | bytes 294920 | tf_op jit(solution)/shard_map/ppermute | solution.py:159
  29.1 5.4 %collective-permute-start.7 = (bf16[4,32,384]{2,1,0:T(8,128)(2,1)S(1)}, bf16[4,32,384]{2,1,0:T(8,128)(2,1)S(1)}, u32[]{:S(2)}, u32[]{:S(2)}) collective-permute-start(bf16[4,32,384]{2,1,0:T(8,128)(2,1)S(1)} %get-tuple-element.69), channel_id=1, source_target_pairs={{0,7},{1,6},{2,5},{3,4},{4,3},{5,2},{6,1},{7,0},{8,15},{9,14},{10,... | collective-permute-start | bytes 294920 | tf_op jit(solution)/shard_map/ppermute | solution.py:159
  29.1 7.3 %collective-permute-start.8 = (bf16[4,32,384]{2,1,0:T(8,128)(2,1)S(1)}, bf16[4,32,384]{2,1,0:T(8,128)(2,1)S(1)}, u32[]{:S(2)}, u32[]{:S(2)}) collective-permute-start(bf16[4,32,384]{2,1,0:T(8,128)(2,1)S(1)} %get-tuple-element.70), channel_id=1, source_target_pairs={{0,4},{1,5},{2,6},{3,7},{4,0},{5,1},{6,2},{7,3},{8,12},{9,13},{10,... | collective-permute-start | bytes 294920 | tf_op jit(solution)/shard_map/ppermute | solution.py:159
  29.6 7.1 %collective-permute-start.9 = (bf16[4,32,384]{2,1,0:T(8,128)(2,1)S(1)}, bf16[4,32,384]{2,1,0:T(8,128)(2,1)S(1)}, u32[]{:S(2)}, u32[]{:S(2)}) collective-permute-start(bf16[4,32,384]{2,1,0:T(8,128)(2,1)S(1)} %get-tuple-element.71), channel_id=1, source_target_pairs={{0,2},{1,3},{2,0},{3,1},{4,6},{5,7},{6,4},{7,5},{8,10},{9,11},{10,... | collective-permute-start | bytes 294920 | tf_op jit(solution)/shard_map/ppermute | solution.py:159
  30.1 8.3 %collective-permute-start.10 = (bf16[4,32,384]{2,1,0:T(8,128)(2,1)S(1)}, bf16[4,32,384]{2,1,0:T(8,128)(2,1)S(1)}, u32[]{:S(2)}, u32[]{:S(2)}) collective-permute-start(bf16[4,32,384]{2,1,0:T(8,128)(2,1)S(1)} %get-tuple-element.72), channel_id=1, source_target_pairs={{0,5},{1,4},{2,7},{3,6},{4,1},{5,0},{6,3},{7,2},{8,13},{9,12},{10,... | collective-permute-start | bytes 294920 | tf_op jit(solution)/shard_map/ppermute | solution.py:159
  32.2 6.2 %collective-permute-start.11 = (bf16[4,32,384]{2,1,0:T(8,128)(2,1)S(1)}, bf16[4,32,384]{2,1,0:T(8,128)(2,1)S(1)}, u32[]{:S(2)}, u32[]{:S(2)}) collective-permute-start(bf16[4,32,384]{2,1,0:T(8,128)(2,1)S(1)} %get-tuple-element.73), channel_id=1, source_target_pairs={{0,3},{1,2},{2,1},{3,0},{4,7},{5,6},{6,5},{7,4},{8,11},{9,10},{10,... | collective-permute-start | bytes 294920 | tf_op jit(solution)/shard_map/ppermute | solution.py:159
  34.4 4.0 %collective-permute-start.12 = (bf16[4,32,384]{2,1,0:T(8,128)(2,1)S(1)}, bf16[4,32,384]{2,1,0:T(8,128)(2,1)S(1)}, u32[]{:S(2)}, u32[]{:S(2)}) collective-permute-start(bf16[4,32,384]{2,1,0:T(8,128)(2,1)S(1)} %get-tuple-element.74), channel_id=1, source_target_pairs={{0,1},{1,0},{2,3},{3,2},{4,5},{5,4},{6,7},{7,6},{8,9},{9,8},{10,11... | collective-permute-start | bytes 294920 | tf_op jit(solution)/shard_map/ppermute | solution.py:159
  39.4 7.4 %collective-permute-start.13 = (bf16[208,128]{1,0:T(8,128)(2,1)S(1)}, bf16[208,128]{1,0:T(8,128)(2,1)S(1)}, u32[]{:S(2)}, u32[]{:S(2)}) collective-permute-start(bf16[208,128]{1,0:T(8,128)(2,1)S(1)} %get-tuple-element.83), channel_id=1, source_target_pairs={{0,16},{8,24},{16,0},{24,8},{1,17},{9,25},{17,1},{25,9},{2,18},{10... | collective-permute-start | bytes 159752 | tf_op jit(solution)/shard_map/ppermute | solution.py:159
  42.4 6.0 %collective-permute-start.14 = (bf16[208,128]{1,0:T(8,128)(2,1)S(1)}, bf16[208,128]{1,0:T(8,128)(2,1)S(1)}, u32[]{:S(2)}, u32[]{:S(2)}) collective-permute-start(bf16[208,128]{1,0:T(8,128)(2,1)S(1)} %get-tuple-element.84), channel_id=1, source_target_pairs={{0,24},{8,16},{16,8},{24,0},{1,25},{9,17},{17,9},{25,1},{2,26},{10... | collective-permute-start | bytes 159752 | tf_op jit(solution)/shard_map/ppermute | solution.py:159
  43.8 4.7 %collective-permute-start.15 = (bf16[208,128]{1,0:T(8,128)(2,1)S(1)}, bf16[208,128]{1,0:T(8,128)(2,1)S(1)}, u32[]{:S(2)}, u32[]{:S(2)}) collective-permute-start(bf16[208,128]{1,0:T(8,128)(2,1)S(1)} %get-tuple-element.85), channel_id=1, source_target_pairs={{0,8},{8,0},{16,24},{24,16},{1,9},{9,1},{17,25},{25,17},{2,10},{10... | collective-permute-start | bytes 159752 | tf_op jit(solution)/shard_map/ppermute | solution.py:159
  43.9 5.5 %collective-permute-start.16 = (bf16[400,128]{1,0:T(8,128)(2,1)S(1)}, bf16[400,128]{1,0:T(8,128)(2,1)S(1)}, u32[]{:S(2)}, u32[]{:S(2)}) collective-permute-start(bf16[400,128]{1,0:T(8,128)(2,1)S(1)} %get-tuple-element.88), channel_id=1, source_target_pairs={{0,4},{1,5},{2,6},{3,7},{4,0},{5,1},{6,2},{7,3},{8,12},{9,13},{10,... | collective-permute-start | bytes 307208 | tf_op jit(solution)/shard_map/ppermute | solution.py:159
  45.5 4.7 %collective-permute-start.17 = (bf16[400,128]{1,0:T(8,128)(2,1)S(1)}, bf16[400,128]{1,0:T(8,128)(2,1)S(1)}, u32[]{:S(2)}, u32[]{:S(2)}) collective-permute-start(bf16[400,128]{1,0:T(8,128)(2,1)S(1)} %get-tuple-element.89), channel_id=1, source_target_pairs={{0,2},{1,3},{2,0},{3,1},{4,6},{5,7},{6,4},{7,5},{8,10},{9,11},{10,... | collective-permute-start | bytes 307208 | tf_op jit(solution)/shard_map/ppermute | solution.py:159

commit v2 on v1

--- a/solution.py
+++ b/solution.py
@@ -357,9 +357,9 @@
     own, first = lax.optimization_barrier((own, first))
     along_y, along_x, kept = pair_sum(first, came_x, second, came_y)
     came_y, came_x = swapped(along_y, "dp", 4), swapped(along_x, "dp", 2)
-    feature_rows = small_call(feature_sum_kernel, jax.ShapeDtypeStruct((1, 3 * BLK, BLK), jnp.float32), own, *terms, cost=1 << 34)
-    kept, feature_rows = lax.optimization_barrier((kept, feature_rows))
     hidden_rows = unpacked(kept, came_y, came_x)
+    own, hidden_rows = lax.optimization_barrier((own, hidden_rows))
+    feature_rows = small_call(feature_sum_kernel, jax.ShapeDtypeStruct((1, 3 * BLK, BLK), jnp.float32), own, *terms)
     return (feature_rows, hidden_rows)
 
 

time: 51.6 us -> 52.2 us (1.012); the launches traced: 51.2 us -> 52.4 us
  waiting for transfers between devices: 10.6 us -> 11.8 us
    ppermute x18, waiting for transfers between devices: 10.6 us -> 11.8 us  [swapped(): lax.ppermute(shard, axis, [(i, i ^ mask) for i in range(lax.axis_size(axi...]
where the time goes in v2:
time: 52.2 us; the launch traced here: 52.4 us
  starting transfers between devices  22.6 us (43%)
  Pallas kernels  16.5 us (32%)
  waiting for transfers between devices  11.8 us (23%)
  between operations  1.4 us (3%)
    ppermute x18, starting transfers between devices, swapped(): lax.ppermute(shard, axis, [(i, i ^ mask) for i in range(lax.axis_size(axi...  22.6 us
    ppermute x18, waiting for transfers between devices, swapped(): lax.ppermute(shard, axis, [(i, i ^ mask) for i in range(lax.axis_size(axi...  11.8 us
    pallas_call x1, Pallas kernels, relay(): pl.pallas_call(functools.partial(relay_kernel, sections, owners), out_sha...  7.42 us
    pallas_call x2, Pallas kernels, hidden_terms(): pl.pallas_call(functools.partial(hidden_kernel, micro, pairs, scale), out...  4 us
    pallas_call x4, Pallas kernels, small_call(): pl.pallas_call(kernel, out_shape=shapes, in_specs=[VMEM_SPEC] * len(opera...  2.15 us
    pallas_call x1, Pallas kernels, messages(): pl.pallas_call(message_kernel, out_shape=(shape,) * (micro - 1), in_specs...  1.94 us
  transfers between devices with their start and end apart: 18, of which 8 were waited for; matrix products, arithmetic and copies ran while one was open for 0% of the time, Pallas kernels for 24%

profile of v2, /device:TPU:0, one launch (start us, length us, event | category | flops | bytes accessed | tf_op | source)
XLA Modules:
  0.0 52.4 jit_solution(113438558910569377)
XLA Ops:
  1.3 0.0 copy-start
  1.3 0.0 copy-start.1
  1.3 1.9 %shard_map.68 = (bf16[496,128]{1,0:T(8,128)(2,1)}, bf16[496,128]{1,0:T(8,128)(2,1)}, bf16[496,128]{1,0:T(8,128)(2,1)}) custom-call(bf16[4,32,1536]{2,1,0:T(8,128)(2,1)} %own_ref.1, f32[48,128]{1,0:T(8,128)} %bitcast.3, s32[1]{0:T(128)S(6)} %copy.7.repeats_ref, s32[1]{0:T(128)} %bitcast.1.me_ref), custom_call_target="tpu_custom_call" | custom-call | flops 8589934592 | bytes 1048576 | tf_op jit(solution)/shard_map/pallas_call | solution.py:182
  3.2 3.0 %collective-permute-start = (bf16[496,128]{1,0:T(8,128)(2,1)}, bf16[496,128]{1,0:T(8,128)(2,1)S(1)}, u32[]{:S(2)}, u32[]{:S(2)}) collective-permute-start(bf16[496,128]{1,0:T(8,128)(2,1)} %get-tuple-element.50), channel_id=1, source_target_pairs={{0,8},{8,0},{16,24},{24,16},{1,9},{9,1},{17,25},{25,17},{2,10},{10... | collective-permute-start | bytes 380936 | tf_op jit(solution)/shard_map/ppermute | solution.py:159
  6.3 2.6 %collective-permute-start.1 = (bf16[496,128]{1,0:T(8,128)(2,1)}, bf16[496,128]{1,0:T(8,128)(2,1)S(1)}, u32[]{:S(2)}, u32[]{:S(2)}) collective-permute-start(bf16[496,128]{1,0:T(8,128)(2,1)} %get-tuple-element.51), channel_id=1, source_target_pairs={{0,16},{8,24},{16,0},{24,8},{1,17},{9,25},{17,1},{25,9},{2,18},{10... | collective-permute-start | bytes 380936 | tf_op jit(solution)/shard_map/ppermute | solution.py:159
  8.9 0.0 collective-permute-start.2
  8.9 0.0 copy-done
  8.9 0.0 copy-done.1
  8.9 2.0 %shard_map.70 = bf16[4,2,400,128]{3,2,1,0:T(8,128)(2,1)S(1)} custom-call(s32[4]{0:T(128)S(1)} %copy-done.1, s32[1]{0:T(128)S(6)} %xor.3._, bf16[1,4,32,12288]{3,2,1,0:T(8,128)(2,1)S(1)} %copy-done, bf16[1,4,32,12288]{3,2,1,0:T(8,128)(2,1)S(1)} %copy-done), custom_call_target="tpu_custom_call" | custom-call | flops 1048576 | bytes 1024 | tf_op jit(solution)/shard_map/pallas_call | solution.py:80
  10.9 0.0 copy-start.2
  10.9 0.0 copy-start.3
  10.9 0.1 collective-permute-start.3
  11.0 2.0 %shard_map.69.near_ref = bf16[4,2,400,128]{3,2,1,0:T(8,128)(2,1)S(1)} custom-call(s32[4]{0:T(128)S(1)} %copy-done.1, s32[1]{0:T(128)} %bitcast.2._, bf16[1,4,32,12288]{3,2,1,0:T(8,128)(2,1)S(1)} %copy-done, bf16[1,4,32,12288]{3,2,1,0:T(8,128)(2,1)S(1)} %copy-done), custom_call_target="tpu_custom_call" | custom-call | flops 17179869184 | bytes 1024 | tf_op jit(solution)/shard_map/pallas_call | solution.py:80
  13.0 0.3 collective-permute-done.3.came_ref
  13.3 0.2 shard_map.71
  13.5 1.8 %collective-permute-start.4 = (bf16[2,400,128]{2,1,0:T(8,128)(2,1)S(1)}, bf16[2,400,128]{2,1,0:T(8,128)(2,1)S(1)}, u32[]{:S(2)}, u32[]{:S(2)}) collective-permute-start(bf16[2,400,128]{2,1,0:T(8,128)(2,1)S(1)} %get-tuple-element.65), channel_id=1, source_target_pairs={{0,2},{1,3},{2,0},{3,1},{4,6},{5,7},{6,4},{7,5},{8,10},{9,11},{10,... | collective-permute-start | bytes 614408 | tf_op jit(solution)/shard_map/ppermute | solution.py:159
  15.2 1.5 %collective-permute-start.5 = (bf16[2,400,128]{2,1,0:T(8,128)(2,1)S(1)}, bf16[2,400,128]{2,1,0:T(8,128)(2,1)S(1)}, u32[]{:S(2)}, u32[]{:S(2)}) collective-permute-start(bf16[2,400,128]{2,1,0:T(8,128)(2,1)S(1)} %get-tuple-element.66), channel_id=1, source_target_pairs={{0,4},{1,5},{2,6},{3,7},{4,0},{5,1},{6,2},{7,3},{8,12},{9,13},{10,... | collective-permute-start | bytes 614408 | tf_op jit(solution)/shard_map/ppermute | solution.py:159
  16.8 0.1 pad_add_fusion.me_ref
  16.8 0.0 collective-permute-done.refs_0_
  16.8 2.2 %collective-permute-done.1.refs_1_ = bf16[496,128]{1,0:T(8,128)(2,1)S(1)} collective-permute-done((bf16[496,128]{1,0:T(8,128)(2,1)}, bf16[496,128]{1,0:T(8,128)(2,1)S(1)}, u32[]{:S(2)}, u32[]{:S(2)}) %collective-permute-start.1) | collective-permute-done | bytes 127008 | tf_op jit(solution)/shard_map/ppermute | solution.py:159
  19.1 0.0 collective-permute-done.2.refs_2_
  19.1 0.0 copy-done.2
  19.1 0.0 copy-done.3
  19.1 7.4 %shard_map.72 = (bf16[4,32,384]{2,1,0:T(8,128)(2,1)S(1)}, bf16[4,32,384]{2,1,0:T(8,128)(2,1)S(1)}, bf16[4,32,384]{2,1,0:T(8,128)(2,1)S(1)}, bf16[4,32,384]{2,1,0...) custom-call(bf16[4,32,1536]{2,1,0:T(8,128)(2,1)S(1)} %copy-done.2, ...), custom_call_target="tpu_custom_call" | custom-call | flops 2147483648 | bytes 2097152 | tf_op jit(solution)/shard_map/pallas_call | solution.py:262
  26.5 0.0 collective-permute-done.4.came_x_ref
  26.5 0.0 collective-permute-done.5.came_y_ref
  26.6 2.5 %collective-permute-start.6 = (bf16[4,32,384]{2,1,0:T(8,128)(2,1)S(1)}, bf16[4,32,384]{2,1,0:T(8,128)(2,1)S(1)}, u32[]{:S(2)}, u32[]{:S(2)}) collective-permute-start(bf16[4,32,384]{2,1,0:T(8,128)(2,1)S(1)} %get-tuple-element.68), channel_id=1, source_target_pairs={{0,6},{1,7},{2,4},{3,5},{4,2},{5,3},{6,0},{7,1},{8,14},{9,15},{10,... | collective-permute-start | bytes 294920 | tf_op jit(solution)/shard_map/ppermute | solution.py:159
  29.1 0.0 collective-permute-start.7
  29.1 0.5 collective-permute-start.8
  29.6 0.5 %collective-permute-start.9 = (bf16[4,32,384]{2,1,0:T(8,128)(2,1)S(1)}, bf16[4,32,384]{2,1,0:T(8,128)(2,1)S(1)}, u32[]{:S(2)}, u32[]{:S(2)}) collective-permute-start(bf16[4,32,384]{2,1,0:T(8,128)(2,1)S(1)} %get-tuple-element.71), channel_id=1, source_target_pairs={{0,2},{1,3},{2,0},{3,1},{4,6},{5,7},{6,4},{7,5},{8,10},{9,11},{10,... | collective-permute-start | bytes 294920 | tf_op jit(solution)/shard_map/ppermute | solution.py:159
  30.1 2.1 %collective-permute-start.10 = (bf16[4,32,384]{2,1,0:T(8,128)(2,1)S(1)}, bf16[4,32,384]{2,1,0:T(8,128)(2,1)S(1)}, u32[]{:S(2)}, u32[]{:S(2)}) collective-permute-start(bf16[4,32,384]{2,1,0:T(8,128)(2,1)S(1)} %get-tuple-element.72), channel_id=1, source_target_pairs={{0,5},{1,4},{2,7},{3,6},{4,1},{5,0},{6,3},{7,2},{8,13},{9,12},{10,... | collective-permute-start | bytes 294920 | tf_op jit(solution)/shard_map/ppermute | solution.py:159
  32.2 0.0 collective-permute-done.6.refs_1_
  32.2 0.6 %collective-permute-start.11 = (bf16[4,32,384]{2,1,0:T(8,128)(2,1)S(1)}, bf16[4,32,384]{2,1,0:T(8,128)(2,1)S(1)}, u32[]{:S(2)}, u32[]{:S(2)}) collective-permute-start(bf16[4,32,384]{2,1,0:T(8,128)(2,1)S(1)} %get-tuple-element.73), channel_id=1, source_target_pairs={{0,3},{1,2},{2,1},{3,0},{4,7},{5,6},{6,5},{7,4},{8,11},{9,10},{10,... | collective-permute-start | bytes 294920 | tf_op jit(solution)/shard_map/ppermute | solution.py:159
  32.8 1.6 %collective-permute-done.7.refs_2_ = bf16[4,32,384]{2,1,0:T(8,128)(2,1)S(1)} collective-permute-done((bf16[4,32,384]{2,1,0:T(8,128)(2,1)S(1)}, bf16[4,32,384]{2,1,0:T(8,128)(2,1)S(1)}, u32[]{:S(2)}, u32[]{:S(2)}) %collective-permute-start.7) | collective-permute-done | bytes 98336 | tf_op jit(solution)/shard_map/ppermute | solution.py:159
  34.4 0.0 collective-permute-start.12
  34.4 1.9 %collective-permute-done.8.refs_3_ = bf16[4,32,384]{2,1,0:T(8,128)(2,1)S(1)} collective-permute-done((bf16[4,32,384]{2,1,0:T(8,128)(2,1)S(1)}, bf16[4,32,384]{2,1,0:T(8,128)(2,1)S(1)}, u32[]{:S(2)}, u32[]{:S(2)}) %collective-permute-start.8) | collective-permute-done | bytes 98336 | tf_op jit(solution)/shard_map/ppermute | solution.py:159
  36.4 0.3 collective-permute-done.9.refs_4_
  36.7 1.8 %collective-permute-done.10.refs_5_ = bf16[4,32,384]{2,1,0:T(8,128)(2,1)S(1)} collective-permute-done((bf16[4,32,384]{2,1,0:T(8,128)(2,1)S(1)}, bf16[4,32,384]{2,1,0:T(8,128)(2,1)S(1)}, u32[]{:S(2)}, u32[]{:S(2)}) %collective-permute-start.10) | collective-permute-done | bytes 98336 | tf_op jit(solution)/shard_map/ppermute | solution.py:159
  38.4 0.0 collective-permute-done.11.refs_6_
  38.4 0.0 collective-permute-done.12.refs_7_
  38.4 1.0 %shard_map.73 = (f32[208,128]{1,0:T(8,128)S(1)}, bf16[208,128]{1,0:T(8,128)(2,1)S(1)}, bf16[208,128]{1,0:T(8,128)(2,1)S(1)}, bf16[208,128]{1,0:T(8,128)(2,1)S(1)}) custom-call(s32[4]{0:T(128)S(1)} %copy-done.1, s32[1]{0:T(128)} %bitcast.1.me_ref, bf16[4,32,384]{2,1,0:T(8,128)(2,1)S(1)} %get-tuple-element.67.refs_0_, ...), custom_call_target="tpu_custom_call" | custom-call | flops 2147483648 | bytes 1048576 | tf_op jit(solution)/shard_map/pallas_call | solution.py:317
  39.4 0.1 shard_map.74
  39.5 1.6 %collective-permute-start.13 = (bf16[400,128]{1,0:T(8,128)(2,1)S(1)}, bf16[400,128]{1,0:T(8,128)(2,1)S(1)}, u32[]{:S(2)}, u32[]{:S(2)}) collective-permute-start(bf16[400,128]{1,0:T(8,128)(2,1)S(1)} %get-tuple-element.83), channel_id=1, source_target_pairs={{0,4},{1,5},{2,6},{3,7},{4,0},{5,1},{6,2},{7,3},{8,12},{9,13},{10,... | collective-permute-start | bytes 307208 | tf_op jit(solution)/shard_map/ppermute | solution.py:159
  41.1 1.1 %collective-permute-start.14 = (bf16[400,128]{1,0:T(8,128)(2,1)S(1)}, bf16[400,128]{1,0:T(8,128)(2,1)S(1)}, u32[]{:S(2)}, u32[]{:S(2)}) collective-permute-start(bf16[400,128]{1,0:T(8,128)(2,1)S(1)} %get-tuple-element.84), channel_id=1, source_target_pairs={{0,2},{1,3},{2,0},{3,1},{4,6},{5,7},{6,4},{7,5},{8,10},{9,11},{10,... | collective-permute-start | bytes 307208 | tf_op jit(solution)/shard_map/ppermute | solution.py:159
  42.2 3.2 %collective-permute-start.15 = (bf16[208,128]{1,0:T(8,128)(2,1)S(1)}, bf16[208,128]{1,0:T(8,128)(2,1)S(1)}, u32[]{:S(2)}, u32[]{:S(2)}) collective-permute-start(bf16[208,128]{1,0:T(8,128)(2,1)S(1)} %get-tuple-element.86), channel_id=1, source_target_pairs={{0,16},{8,24},{16,0},{24,8},{1,17},{9,25},{17,1},{25,9},{2,18},{10... | collective-permute-start | bytes 159752 | tf_op jit(solution)/shard_map/ppermute | solution.py:159
  45.5 1.3 %collective-permute-start.16 = (bf16[208,128]{1,0:T(8,128)(2,1)S(1)}, bf16[208,128]{1,0:T(8,128)(2,1)S(1)}, u32[]{:S(2)}, u32[]{:S(2)}) collective-permute-start(bf16[208,128]{1,0:T(8,128)(2,1)S(1)} %get-tuple-element.87), channel_id=1, source_target_pairs={{0,24},{8,16},{16,8},{24,0},{1,25},{9,17},{17,9},{25,1},{2,26},{10... | collective-permute-start | bytes 159752 | tf_op jit(solution)/shard_map/ppermute | solution.py:159
  46.8 0.0 collective-permute-start.17
  46.8 0.0 collective-permute-done.13.came_y_ref
  46.8 0.0 collective-permute-done.14.came_x_ref
  46.8 1.1 %shard_map.75 = f32[1,1536,128]{2,1,0:T(8,128)} custom-call(f32[2,400,128]{2,1,0:T(8,128)S(1)} %get-tuple-element.82.kept_ref, bf16[400,128]{1,0:T(8,128)(2,1)S(1)} %collective-permute-done.13.came_y_ref, bf16[400,128]{1,0:T(8,128)(2,1)S(1)} %collective-permute-done.14.came_x_ref), custom_call_target="tpu_custom_call" | custom-call | flops 1048576 | bytes 1024 | tf_op jit(solution)/shard_map/pallas_call | solution.py:95
  47.9 0.2 collective-permute-done.15.refs_1_
  48.1 3.4 %collective-permute-done.16.refs_2_ = bf16[208,128]{1,0:T(8,128)(2,1)S(1)} collective-permute-done((bf16[208,128]{1,0:T(8,128)(2,1)S(1)}, bf16[208,128]{1,0:T(8,128)(2,1)S(1)}, u32[]{:S(2)}, u32[]{:S(2)}) %collective-permute-start.16) | collective-permute-done | bytes 53280 | tf_op jit(solution)/shard_map/ppermute | solution.py:159
  51.5 0.0 collective-permute-done.17.refs_3_
  51.5 0.8 %shard_map.76 = f32[1,384,128]{2,1,0:T(8,128)} custom-call(f32[208,128]{1,0:T(8,128)S(1)} %get-tuple-element.85.refs_0_, bf16[208,128]{1,0:T(8,128)(2,1)S(1)} %collective-permute-done.15.refs_1_, bf16[208,128]{1,0:T(8,128)(2,1)S(1)} %collective-permute-done.16.refs_2_, bf16[208,128]{1,0:T(8,128)(2,1)S(1)} %collective-permute-done.17.refs_3_), custom_call_target="tpu_custom_call" | custom-call | flops 1048576 | bytes 1024 | tf_op jit(solution)/shard_map/pallas_call | solution.py:95
Async XLA Ops:
  1.3 7.6 %copy-start = (bf16[1,4,32,12288]{3,2,1,0:T(8,128)(2,1)S(1)}, bf16[1,4,32,12288]{3,2,1,0:T(8,128)(2,1)}, u32[]{:S(2)}) copy-start(bf16[1,4,32,12288]{3,2,1,0:T(8,128)(2,1)} %refs_1_.3) | copy-start | bytes 9437188
  1.3 7.6 %copy-start.1 = (s32[4]{0:T(128)S(1)}, s32[4]{0:T(128)}, u32[]{:S(2)}) copy-start(s32[4]{0:T(128)} %order_ref.2) | copy-start | bytes 52
  3.2 13.6 %collective-permute-start = (bf16[496,128]{1,0:T(8,128)(2,1)}, bf16[496,128]{1,0:T(8,128)(2,1)S(1)}, u32[]{:S(2)}, u32[]{:S(2)}) collective-permute-start(bf16[496,128]{1,0:T(8,128)(2,1)} %get-tuple-element.50), channel_id=1, source_target_pairs={{0,8},{8,0},{16,24},{24,16},{1,9},{9,1},{17,25},{25,17},{2,10},{10... | collective-permute-start | bytes 380936 | tf_op jit(solution)/shard_map/ppermute | solution.py:159
  6.3 12.8 %collective-permute-start.1 = (bf16[496,128]{1,0:T(8,128)(2,1)}, bf16[496,128]{1,0:T(8,128)(2,1)S(1)}, u32[]{:S(2)}, u32[]{:S(2)}) collective-permute-start(bf16[496,128]{1,0:T(8,128)(2,1)} %get-tuple-element.51), channel_id=1, source_target_pairs={{0,16},{8,24},{16,0},{24,8},{1,17},{9,25},{17,1},{25,9},{2,18},{10... | collective-permute-start | bytes 380936 | tf_op jit(solution)/shard_map/ppermute | solution.py:159
  8.9 10.2 %collective-permute-start.2 = (bf16[496,128]{1,0:T(8,128)(2,1)}, bf16[496,128]{1,0:T(8,128)(2,1)S(1)}, u32[]{:S(2)}, u32[]{:S(2)}) collective-permute-start(bf16[496,128]{1,0:T(8,128)(2,1)} %get-tuple-element.52), channel_id=1, source_target_pairs={{0,24},{8,16},{16,8},{24,0},{1,25},{9,17},{17,9},{25,1},{2,26},{10... | collective-permute-start | bytes 380936 | tf_op jit(solution)/shard_map/ppermute | solution.py:159
  10.9 8.2 %copy-start.2 = (bf16[4,32,1536]{2,1,0:T(8,128)(2,1)S(1)}, bf16[4,32,1536]{2,1,0:T(8,128)(2,1)}, u32[]{:S(2)}) copy-start(bf16[4,32,1536]{2,1,0:T(8,128)(2,1)} %own_ref.1) | copy-start | bytes 1179652
  10.9 8.2 %copy-start.3 = (f32[1,6144]{1,0:T(1,128)S(1)}, f32[1,6144]{1,0:T(1,128)}, u32[]{:S(2)}) copy-start(f32[1,6144]{1,0:T(1,128)} %param.6) | copy-start | bytes 73732
  10.9 2.4 %collective-permute-start.3 = (bf16[4,2,400,128]{3,2,1,0:T(8,128)(2,1)S(1)}, bf16[4,2,400,128]{3,2,1,0:T(8,128)(2,1)S(1)}, u32[]{:S(2)}, u32[]{:S(2)}) collective-permute-start(bf16[4,2,400,128]{3,2,1,0:T(8,128)(2,1)S(1)} %shard_map.70), channel_id=1, source_target_pairs={{0,1},{1,0},{2,3},{3,2},{4,5},{5,4},{6,7},{7,6},{8,9},{9,8},{10,11... | collective-permute-start | bytes 2457608 | tf_op jit(solution)/shard_map/ppermute | solution.py:159
  13.5 13.1 %collective-permute-start.4 = (bf16[2,400,128]{2,1,0:T(8,128)(2,1)S(1)}, bf16[2,400,128]{2,1,0:T(8,128)(2,1)S(1)}, u32[]{:S(2)}, u32[]{:S(2)}) collective-permute-start(bf16[2,400,128]{2,1,0:T(8,128)(2,1)S(1)} %get-tuple-element.65), channel_id=1, source_target_pairs={{0,2},{1,3},{2,0},{3,1},{4,6},{5,7},{6,4},{7,5},{8,10},{9,11},{10,... | collective-permute-start | bytes 614408 | tf_op jit(solution)/shard_map/ppermute | solution.py:159
  15.2 11.3 %collective-permute-start.5 = (bf16[2,400,128]{2,1,0:T(8,128)(2,1)S(1)}, bf16[2,400,128]{2,1,0:T(8,128)(2,1)S(1)}, u32[]{:S(2)}, u32[]{:S(2)}) collective-permute-start(bf16[2,400,128]{2,1,0:T(8,128)(2,1)S(1)} %get-tuple-element.66), channel_id=1, source_target_pairs={{0,4},{1,5},{2,6},{3,7},{4,0},{5,1},{6,2},{7,3},{8,12},{9,13},{10,... | collective-permute-start | bytes 614408 | tf_op jit(solution)/shard_map/ppermute | solution.py:159
  26.6 5.7 %collective-permute-start.6 = (bf16[4,32,384]{2,1,0:T(8,128)(2,1)S(1)}, bf16[4,32,384]{2,1,0:T(8,128)(2,1)S(1)}, u32[]{:S(2)}, u32[]{:S(2)}) collective-permute-start(bf16[4,32,384]{2,1,0:T(8,128)(2,1)S(1)} %get-tuple-element.68), channel_id=1, source_target_pairs={{0,6},{1,7},{2,4},{3,5},{4,2},{5,3},{6,0},{7,1},{8,14},{9,15},{10,... | collective-permute-start | bytes 294920 | tf_op jit(solution)/shard_map/ppermute | solution.py:159
  29.1 5.4 %collective-permute-start.7 = (bf16[4,32,384]{2,1,0:T(8,128)(2,1)S(1)}, bf16[4,32,384]{2,1,0:T(8,128)(2,1)S(1)}, u32[]{:S(2)}, u32[]{:S(2)}) collective-permute-start(bf16[4,32,384]{2,1,0:T(8,128)(2,1)S(1)} %get-tuple-element.69), channel_id=1, source_target_pairs={{0,7},{1,6},{2,5},{3,4},{4,3},{5,2},{6,1},{7,0},{8,15},{9,14},{10,... | collective-permute-start | bytes 294920 | tf_op jit(solution)/shard_map/ppermute | solution.py:159
  29.1 7.3 %collective-permute-start.8 = (bf16[4,32,384]{2,1,0:T(8,128)(2,1)S(1)}, bf16[4,32,384]{2,1,0:T(8,128)(2,1)S(1)}, u32[]{:S(2)}, u32[]{:S(2)}) collective-permute-start(bf16[4,32,384]{2,1,0:T(8,128)(2,1)S(1)} %get-tuple-element.70), channel_id=1, source_target_pairs={{0,4},{1,5},{2,6},{3,7},{4,0},{5,1},{6,2},{7,3},{8,12},{9,13},{10,... | collective-permute-start | bytes 294920 | tf_op jit(solution)/shard_map/ppermute | solution.py:159
  29.6 7.1 %collective-permute-start.9 = (bf16[4,32,384]{2,1,0:T(8,128)(2,1)S(1)}, bf16[4,32,384]{2,1,0:T(8,128)(2,1)S(1)}, u32[]{:S(2)}, u32[]{:S(2)}) collective-permute-start(bf16[4,32,384]{2,1,0:T(8,128)(2,1)S(1)} %get-tuple-element.71), channel_id=1, source_target_pairs={{0,2},{1,3},{2,0},{3,1},{4,6},{5,7},{6,4},{7,5},{8,10},{9,11},{10,... | collective-permute-start | bytes 294920 | tf_op jit(solution)/shard_map/ppermute | solution.py:159
  30.1 8.3 %collective-permute-start.10 = (bf16[4,32,384]{2,1,0:T(8,128)(2,1)S(1)}, bf16[4,32,384]{2,1,0:T(8,128)(2,1)S(1)}, u32[]{:S(2)}, u32[]{:S(2)}) collective-permute-start(bf16[4,32,384]{2,1,0:T(8,128)(2,1)S(1)} %get-tuple-element.72), channel_id=1, source_target_pairs={{0,5},{1,4},{2,7},{3,6},{4,1},{5,0},{6,3},{7,2},{8,13},{9,12},{10,... | collective-permute-start | bytes 294920 | tf_op jit(solution)/shard_map/ppermute | solution.py:159
  32.2 6.2 %collective-permute-start.11 = (bf16[4,32,384]{2,1,0:T(8,128)(2,1)S(1)}, bf16[4,32,384]{2,1,0:T(8,128)(2,1)S(1)}, u32[]{:S(2)}, u32[]{:S(2)}) collective-permute-start(bf16[4,32,384]{2,1,0:T(8,128)(2,1)S(1)} %get-tuple-element.73), channel_id=1, source_target_pairs={{0,3},{1,2},{2,1},{3,0},{4,7},{5,6},{6,5},{7,4},{8,11},{9,10},{10,... | collective-permute-start | bytes 294920 | tf_op jit(solution)/shard_map/ppermute | solution.py:159
  34.4 4.0 %collective-permute-start.12 = (bf16[4,32,384]{2,1,0:T(8,128)(2,1)S(1)}, bf16[4,32,384]{2,1,0:T(8,128)(2,1)S(1)}, u32[]{:S(2)}, u32[]{:S(2)}) collective-permute-start(bf16[4,32,384]{2,1,0:T(8,128)(2,1)S(1)} %get-tuple-element.74), channel_id=1, source_target_pairs={{0,1},{1,0},{2,3},{3,2},{4,5},{5,4},{6,7},{7,6},{8,9},{9,8},{10,11... | collective-permute-start | bytes 294920 | tf_op jit(solution)/shard_map/ppermute | solution.py:159
  39.5 7.3 %collective-permute-start.13 = (bf16[400,128]{1,0:T(8,128)(2,1)S(1)}, bf16[400,128]{1,0:T(8,128)(2,1)S(1)}, u32[]{:S(2)}, u32[]{:S(2)}) collective-permute-start(bf16[400,128]{1,0:T(8,128)(2,1)S(1)} %get-tuple-element.83), channel_id=1, source_target_pairs={{0,4},{1,5},{2,6},{3,7},{4,0},{5,1},{6,2},{7,3},{8,12},{9,13},{10,... | collective-permute-start | bytes 307208 | tf_op jit(solution)/shard_map/ppermute | solution.py:159
  41.1 5.7 %collective-permute-start.14 = (bf16[400,128]{1,0:T(8,128)(2,1)S(1)}, bf16[400,128]{1,0:T(8,128)(2,1)S(1)}, u32[]{:S(2)}, u32[]{:S(2)}) collective-permute-start(bf16[400,128]{1,0:T(8,128)(2,1)S(1)} %get-tuple-element.84), channel_id=1, source_target_pairs={{0,2},{1,3},{2,0},{3,1},{4,6},{5,7},{6,4},{7,5},{8,10},{9,11},{10,... | collective-permute-start | bytes 307208 | tf_op jit(solution)/shard_map/ppermute | solution.py:159
  42.2 5.8 %collective-permute-start.15 = (bf16[208,128]{1,0:T(8,128)(2,1)S(1)}, bf16[208,128]{1,0:T(8,128)(2,1)S(1)}, u32[]{:S(2)}, u32[]{:S(2)}) collective-permute-start(bf16[208,128]{1,0:T(8,128)(2,1)S(1)} %get-tuple-element.86), channel_id=1, source_target_pairs={{0,16},{8,24},{16,0},{24,8},{1,17},{9,25},{17,1},{25,9},{2,18},{10... | collective-permute-start | bytes 159752 | tf_op jit(solution)/shard_map/ppermute | solution.py:159
  45.5 6.0 %collective-permute-start.16 = (bf16[208,128]{1,0:T(8,128)(2,1)S(1)}, bf16[208,128]{1,0:T(8,128)(2,1)S(1)}, u32[]{:S(2)}, u32[]{:S(2)}) collective-permute-start(bf16[208,128]{1,0:T(8,128)(2,1)S(1)} %get-tuple-element.87), channel_id=1, source_target_pairs={{0,24},{8,16},{16,8},{24,0},{1,25},{9,17},{17,9},{25,1},{2,26},{10... | collective-permute-start | bytes 159752 | tf_op jit(solution)/shard_map/ppermute | solution.py:159
  46.8 4.7 %collective-permute-start.17 = (bf16[208,128]{1,0:T(8,128)(2,1)S(1)}, bf16[208,128]{1,0:T(8,128)(2,1)S(1)}, u32[]{:S(2)}, u32[]{:S(2)}) collective-permute-start(bf16[208,128]{1,0:T(8,128)(2,1)S(1)} %get-tuple-element.88), channel_id=1, source_target_pairs={{0,8},{8,0},{16,24},{24,16},{1,9},{9,1},{17,25},{25,17},{2,10},{10... | collective-permute-start | bytes 159752 | tf_op jit(solution)/shard_map/ppermute | solution.py:159

commit v3 on v1

--- a/solution.py
+++ b/solution.py
@@ -11,6 +11,7 @@
 GWIN = 12288
 BLK = 128
 VMEM_LIMIT = 16 * 1024 * 1024
+FAR_FIRST = (2, 3, 1)
 ROOT = 0.7978845608028654
 
 SMEM_SPEC = pl.BlockSpec(memory_space=pltpu.SMEM)
@@ -167,7 +168,7 @@
     low = (gain - high.astype(jnp.float32)).astype(jnp.bfloat16)
     count = jnp.full((16, BLK), repeats_ref[0], jnp.int32).astype(jnp.float32).astype(jnp.bfloat16)
     at = chunks * rows
-    for mask, out_ref in enumerate(out_refs, 1):
+    for mask, out_ref in zip(FAR_FIRST, out_refs):
         target = jnp.bitwise_xor(me_ref[0], mask)
         for chunk in range(chunks):
             out_ref[chunk * rows:(chunk + 1) * rows] = in_ref[target, :, chunk * BLK:(chunk + 1) * BLK]
@@ -209,7 +210,7 @@
         value = own_ref[me, :, chunk * BLK:(chunk + 1) * BLK].astype(jnp.float32)
         held[me * part + chunk] = value
         total = total + value
-    for mask, ref in enumerate(received, 1):
+    for mask, ref in zip(FAR_FIRST, received):
         source = jnp.bitwise_xor(me, mask)
         gains[source, :chunks] = ref[at:at + chunks].astype(jnp.float32) + ref[at + chunks:at + 2 * chunks].astype(jnp.float32)
         gains[source, chunks:] = ref[at + 2 * chunks:].astype(jnp.float32)[:8]
@@ -304,7 +305,7 @@
 def feature_kernel(micro, scale, order_ref, me_ref, *refs):
     in_refs, (own_ref, *out_refs) = refs[:-micro], refs[-micro:]
     weight = batch_weight(order_ref, me_ref[0], micro) * scale
-    for mask, out_ref in enumerate([own_ref] + out_refs):
+    for mask, out_ref in zip((0,) + FAR_FIRST, [own_ref] + out_refs):
         s = jnp.bitwise_xor(me_ref[0], mask)
         blocks = []
         for at in range(0, 3 * BLK, BLK):
@@ -340,8 +341,7 @@
     plane, place = lax.axis_index("section").reshape(1), lax.axis_index("dp").reshape(1)
     me = jnp.concatenate([plane, place])
     told, order = lax.optimization_barrier((messages(inputs, gain, repeats, plane), order))
-    pieces = {mask: swapped(told[mask - 1], "section", mask) for mask in (2, 3, 1)}
-    pieces = tuple(pieces[mask] for mask in (1, 2, 3))
+    pieces = tuple(swapped(one, "section", mask) for mask, one in zip(FAR_FIRST, told))
 
     came = swapped(hidden_terms(order, hidden_grad, place ^ 1, dp_count, scale, 1 << 20), "dp", 1)
     near = hidden_terms(order, hidden_grad, place, dp_count, scale, 1 << 34)
@@ -353,7 +353,7 @@
     feats, came_x, came_y = lax.optimization_barrier((feats, came_x, came_y))
     gathered = [feats[0]] + [swapped(feats[mask], "dp", mask) for mask in (6, 7, 4, 2, 5, 3, 1)]
     own, *terms = feature_terms(order, plane, gathered, micro, scale)
-    terms = [swapped(terms[mask - 1], "section", mask) for mask in (2, 3, 1)]
+    terms = [swapped(one, "section", mask) for mask, one in zip(FAR_FIRST, terms)]
     own, first = lax.optimization_barrier((own, first))
     along_y, along_x, kept = pair_sum(first, came_x, second, came_y)
     came_y, came_x = swapped(along_y, "dp", 4), swapped(along_x, "dp", 2)

time: 51.6 us -> 50.2 us (0.973); the launches traced: 51.2 us -> 50.9 us
  waiting for transfers between devices: 10.6 us -> 9.24 us
  Pallas kernels: 16.5 us -> 17.1 us
    ppermute x18, waiting for transfers between devices: 10.6 us -> 9.24 us  [swapped(): lax.ppermute(shard, axis, [(i, i ^ mask) for i in range(lax.axis_size(axi...]
    pallas_call x1, Pallas kernels: 7.4 us -> 7.98 us  [relay(): pl.pallas_call(functools.partial(relay_kernel, sections, owners), out_sha...]
  transfers between devices with their start and end apart: 18 -> 18, of which waited for: 8 -> 9; matrix products, arithmetic and copies ran while one was open for 0% -> 0% of each run, Pallas kernels for 24% -> 26%
where the time goes in v3:
time: 50.2 us; the launch traced here: 50.9 us
  starting transfers between devices  23.1 us (46%)
  Pallas kernels  17.1 us (34%)
  waiting for transfers between devices  9.24 us (18%)
  between operations  1.39 us (3%)
    ppermute x18, starting transfers between devices, swapped(): lax.ppermute(shard, axis, [(i, i ^ mask) for i in range(lax.axis_size(axi...  23.1 us
    ppermute x18, waiting for transfers between devices, swapped(): lax.ppermute(shard, axis, [(i, i ^ mask) for i in range(lax.axis_size(axi...  9.24 us
    pallas_call x1, Pallas kernels, relay(): pl.pallas_call(functools.partial(relay_kernel, sections, owners), out_sha...  7.98 us
    pallas_call x2, Pallas kernels, hidden_terms(): pl.pallas_call(functools.partial(hidden_kernel, micro, pairs, scale), out...  3.99 us
    pallas_call x4, Pallas kernels, small_call(): pl.pallas_call(kernel, out_shape=shapes, in_specs=[VMEM_SPEC] * len(opera...  2.16 us
    pallas_call x1, Pallas kernels, messages(): pl.pallas_call(message_kernel, out_shape=(shape,) * (micro - 1), in_specs...  1.94 us
    pallas_call x1, Pallas kernels, feature_terms(): pl.pallas_call(functools.partial(feature_kernel, micro, scale), out_shape...  1.01 us
  transfers between devices with their start and end apart: 18, of which 9 were waited for; matrix products, arithmetic and copies ran while one was open for 0% of the time, Pallas kernels for 26%

profile of v3, /device:TPU:0, one launch (start us, length us, event | category | flops | bytes accessed | tf_op | source)
XLA Modules:
  0.0 50.9 jit_solution(14369340273359464665)
XLA Ops:
  1.3 0.0 copy-start
  1.3 0.0 copy-start.1
  1.3 1.9 %shard_map.68 = (bf16[496,128]{1,0:T(8,128)(2,1)}, bf16[496,128]{1,0:T(8,128)(2,1)}, bf16[496,128]{1,0:T(8,128)(2,1)}) custom-call(bf16[4,32,1536]{2,1,0:T(8,128)(2,1)} %own_ref.1, f32[48,128]{1,0:T(8,128)} %bitcast.3, s32[1]{0:T(128)S(6)} %copy.7.repeats_ref, s32[1]{0:T(128)} %bitcast.1.me_ref), custom_call_target="tpu_custom_call" | custom-call | flops 8589934592 | bytes 1048576 | tf_op jit(solution)/shard_map/pallas_call | solution.py:183
  3.2 4.0 %collective-permute-start = (bf16[496,128]{1,0:T(8,128)(2,1)}, bf16[496,128]{1,0:T(8,128)(2,1)S(1)}, u32[]{:S(2)}, u32[]{:S(2)}) collective-permute-start(bf16[496,128]{1,0:T(8,128)(2,1)} %get-tuple-element.50), channel_id=1, source_target_pairs={{0,16},{8,24},{16,0},{24,8},{1,17},{9,25},{17,1},{25,9},{2,18},{10... | collective-permute-start | bytes 380936 | tf_op jit(solution)/shard_map/ppermute | solution.py:160
  7.3 1.3 %collective-permute-start.1 = (bf16[496,128]{1,0:T(8,128)(2,1)}, bf16[496,128]{1,0:T(8,128)(2,1)S(1)}, u32[]{:S(2)}, u32[]{:S(2)}) collective-permute-start(bf16[496,128]{1,0:T(8,128)(2,1)} %get-tuple-element.51), channel_id=1, source_target_pairs={{0,24},{8,16},{16,8},{24,0},{1,25},{9,17},{17,9},{25,1},{2,26},{10... | collective-permute-start | bytes 380936 | tf_op jit(solution)/shard_map/ppermute | solution.py:160
  8.6 0.2 collective-permute-start.2
  8.9 0.0 copy-done
  8.9 0.0 copy-done.1
  8.9 2.0 %shard_map.70 = bf16[4,2,400,128]{3,2,1,0:T(8,128)(2,1)S(1)} custom-call(s32[4]{0:T(128)S(1)} %copy-done.1, s32[1]{0:T(128)S(6)} %xor.3._, bf16[1,4,32,12288]{3,2,1,0:T(8,128)(2,1)S(1)} %copy-done, bf16[1,4,32,12288]{3,2,1,0:T(8,128)(2,1)S(1)} %copy-done), custom_call_target="tpu_custom_call" | custom-call | flops 1048576 | bytes 1024 | tf_op jit(solution)/shard_map/pallas_call | solution.py:81
  10.9 0.0 copy-start.2
  10.9 0.0 copy-start.3
  10.9 0.1 collective-permute-start.3
  11.0 2.0 %shard_map.69.near_ref = bf16[4,2,400,128]{3,2,1,0:T(8,128)(2,1)S(1)} custom-call(s32[4]{0:T(128)S(1)} %copy-done.1, s32[1]{0:T(128)} %bitcast.2._, bf16[1,4,32,12288]{3,2,1,0:T(8,128)(2,1)S(1)} %copy-done, bf16[1,4,32,12288]{3,2,1,0:T(8,128)(2,1)S(1)} %copy-done), custom_call_target="tpu_custom_call" | custom-call | flops 17179869184 | bytes 1024 | tf_op jit(solution)/shard_map/pallas_call | solution.py:81
  13.0 0.3 collective-permute-done.3.came_ref
  13.3 0.2 shard_map.71
  13.5 1.6 %collective-permute-start.4 = (bf16[2,400,128]{2,1,0:T(8,128)(2,1)S(1)}, bf16[2,400,128]{2,1,0:T(8,128)(2,1)S(1)}, u32[]{:S(2)}, u32[]{:S(2)}) collective-permute-start(bf16[2,400,128]{2,1,0:T(8,128)(2,1)S(1)} %get-tuple-element.65), channel_id=1, source_target_pairs={{0,2},{1,3},{2,0},{3,1},{4,6},{5,7},{6,4},{7,5},{8,10},{9,11},{10,... | collective-permute-start | bytes 614408 | tf_op jit(solution)/shard_map/ppermute | solution.py:160
  15.0 1.5 %collective-permute-start.5 = (bf16[2,400,128]{2,1,0:T(8,128)(2,1)S(1)}, bf16[2,400,128]{2,1,0:T(8,128)(2,1)S(1)}, u32[]{:S(2)}, u32[]{:S(2)}) collective-permute-start(bf16[2,400,128]{2,1,0:T(8,128)(2,1)S(1)} %get-tuple-element.66), channel_id=1, source_target_pairs={{0,4},{1,5},{2,6},{3,7},{4,0},{5,1},{6,2},{7,3},{8,12},{9,13},{10,... | collective-permute-start | bytes 614408 | tf_op jit(solution)/shard_map/ppermute | solution.py:160
  16.6 0.1 pad_add_fusion.me_ref
  16.6 0.6 %collective-permute-done.refs_0_ = bf16[496,128]{1,0:T(8,128)(2,1)S(1)} collective-permute-done((bf16[496,128]{1,0:T(8,128)(2,1)}, bf16[496,128]{1,0:T(8,128)(2,1)S(1)}, u32[]{:S(2)}, u32[]{:S(2)}) %collective-permute-start) | collective-permute-done | bytes 127008 | tf_op jit(solution)/shard_map/ppermute | solution.py:160
  17.2 0.0 collective-permute-done.1.refs_1_
  17.2 0.5 collective-permute-done.2.refs_2_
  17.7 0.0 copy-done.2
  17.7 0.0 copy-done.3
  17.7 8.0 %shard_map.72 = (bf16[4,32,384]{2,1,0:T(8,128)(2,1)S(1)}, bf16[4,32,384]{2,1,0:T(8,128)(2,1)S(1)}, bf16[4,32,384]{2,1,0:T(8,128)(2,1)S(1)}, bf16[4,32,384]{2,1,0...) custom-call(bf16[4,32,1536]{2,1,0:T(8,128)(2,1)S(1)} %copy-done.2, ...), custom_call_target="tpu_custom_call" | custom-call | flops 2147483648 | bytes 2097152 | tf_op jit(solution)/shard_map/pallas_call | solution.py:263
  25.7 0.0 collective-permute-done.4.came_x_ref
  25.7 0.0 collective-permute-done.5.came_y_ref
  25.7 2.6 %collective-permute-start.6 = (bf16[4,32,384]{2,1,0:T(8,128)(2,1)S(1)}, bf16[4,32,384]{2,1,0:T(8,128)(2,1)S(1)}, u32[]{:S(2)}, u32[]{:S(2)}) collective-permute-start(bf16[4,32,384]{2,1,0:T(8,128)(2,1)S(1)} %get-tuple-element.68), channel_id=1, source_target_pairs={{0,6},{1,7},{2,4},{3,5},{4,2},{5,3},{6,0},{7,1},{8,14},{9,15},{10,... | collective-permute-start | bytes 294920 | tf_op jit(solution)/shard_map/ppermute | solution.py:160
  28.3 0.0 collective-permute-start.7
  28.3 0.5 collective-permute-start.8
  28.8 0.5 collective-permute-start.9
  29.3 2.2 %collective-permute-start.10 = (bf16[4,32,384]{2,1,0:T(8,128)(2,1)S(1)}, bf16[4,32,384]{2,1,0:T(8,128)(2,1)S(1)}, u32[]{:S(2)}, u32[]{:S(2)}) collective-permute-start(bf16[4,32,384]{2,1,0:T(8,128)(2,1)S(1)} %get-tuple-element.72), channel_id=1, source_target_pairs={{0,5},{1,4},{2,7},{3,6},{4,1},{5,0},{6,3},{7,2},{8,13},{9,12},{10,... | collective-permute-start | bytes 294920 | tf_op jit(solution)/shard_map/ppermute | solution.py:160
  31.4 0.0 collective-permute-done.6.refs_1_
  31.4 0.6 %collective-permute-start.11 = (bf16[4,32,384]{2,1,0:T(8,128)(2,1)S(1)}, bf16[4,32,384]{2,1,0:T(8,128)(2,1)S(1)}, u32[]{:S(2)}, u32[]{:S(2)}) collective-permute-start(bf16[4,32,384]{2,1,0:T(8,128)(2,1)S(1)} %get-tuple-element.73), channel_id=1, source_target_pairs={{0,3},{1,2},{2,1},{3,0},{4,7},{5,6},{6,5},{7,4},{8,11},{9,10},{10,... | collective-permute-start | bytes 294920 | tf_op jit(solution)/shard_map/ppermute | solution.py:160
  32.1 1.5 %collective-permute-done.7.refs_2_ = bf16[4,32,384]{2,1,0:T(8,128)(2,1)S(1)} collective-permute-done((bf16[4,32,384]{2,1,0:T(8,128)(2,1)S(1)}, bf16[4,32,384]{2,1,0:T(8,128)(2,1)S(1)}, u32[]{:S(2)}, u32[]{:S(2)}) %collective-permute-start.7) | collective-permute-done | bytes 98336 | tf_op jit(solution)/shard_map/ppermute | solution.py:160
  33.6 0.0 collective-permute-start.12
  33.6 2.0 %collective-permute-done.8.refs_3_ = bf16[4,32,384]{2,1,0:T(8,128)(2,1)S(1)} collective-permute-done((bf16[4,32,384]{2,1,0:T(8,128)(2,1)S(1)}, bf16[4,32,384]{2,1,0:T(8,128)(2,1)S(1)}, u32[]{:S(2)}, u32[]{:S(2)}) %collective-permute-start.8) | collective-permute-done | bytes 98336 | tf_op jit(solution)/shard_map/ppermute | solution.py:160
  35.5 0.3 collective-permute-done.9.refs_4_
  35.9 1.7 %collective-permute-done.10.refs_5_ = bf16[4,32,384]{2,1,0:T(8,128)(2,1)S(1)} collective-permute-done((bf16[4,32,384]{2,1,0:T(8,128)(2,1)S(1)}, bf16[4,32,384]{2,1,0:T(8,128)(2,1)S(1)}, u32[]{:S(2)}, u32[]{:S(2)}) %collective-permute-start.10) | collective-permute-done | bytes 98336 | tf_op jit(solution)/shard_map/ppermute | solution.py:160
  37.6 0.0 collective-permute-done.11.refs_6_
  37.6 0.0 collective-permute-done.12.refs_7_
  37.6 1.0 %shard_map.73 = (f32[208,128]{1,0:T(8,128)S(1)}, bf16[208,128]{1,0:T(8,128)(2,1)S(1)}, bf16[208,128]{1,0:T(8,128)(2,1)S(1)}, bf16[208,128]{1,0:T(8,128)(2,1)S(1)}) custom-call(s32[4]{0:T(128)S(1)} %copy-done.1, s32[1]{0:T(128)} %bitcast.1.me_ref, bf16[4,32,384]{2,1,0:T(8,128)(2,1)S(1)} %get-tuple-element.67.refs_0_, ...), custom_call_target="tpu_custom_call" | custom-call | flops 2147483648 | bytes 1048576 | tf_op jit(solution)/shard_map/pallas_call | solution.py:318
  38.6 4.0 %collective-permute-start.13 = (bf16[208,128]{1,0:T(8,128)(2,1)S(1)}, bf16[208,128]{1,0:T(8,128)(2,1)S(1)}, u32[]{:S(2)}, u32[]{:S(2)}) collective-permute-start(bf16[208,128]{1,0:T(8,128)(2,1)S(1)} %get-tuple-element.83), channel_id=1, source_target_pairs={{0,16},{8,24},{16,0},{24,8},{1,17},{9,25},{17,1},{25,9},{2,18},{10... | collective-permute-start | bytes 159752 | tf_op jit(solution)/shard_map/ppermute | solution.py:160
  42.6 0.5 %collective-permute-start.14 = (bf16[208,128]{1,0:T(8,128)(2,1)S(1)}, bf16[208,128]{1,0:T(8,128)(2,1)S(1)}, u32[]{:S(2)}, u32[]{:S(2)}) collective-permute-start(bf16[208,128]{1,0:T(8,128)(2,1)S(1)} %get-tuple-element.84), channel_id=1, source_target_pairs={{0,24},{8,16},{16,8},{24,0},{1,25},{9,17},{17,9},{25,1},{2,26},{10... | collective-permute-start | bytes 159752 | tf_op jit(solution)/shard_map/ppermute | solution.py:160
  43.2 0.1 collective-permute-start.15
  43.3 0.1 shard_map.74
  43.4 1.8 %collective-permute-start.16 = (bf16[400,128]{1,0:T(8,128)(2,1)S(1)}, bf16[400,128]{1,0:T(8,128)(2,1)S(1)}, u32[]{:S(2)}, u32[]{:S(2)}) collective-permute-start(bf16[400,128]{1,0:T(8,128)(2,1)S(1)} %get-tuple-element.88), channel_id=1, source_target_pairs={{0,4},{1,5},{2,6},{3,7},{4,0},{5,1},{6,2},{7,3},{8,12},{9,13},{10,... | collective-permute-start | bytes 307208 | tf_op jit(solution)/shard_map/ppermute | solution.py:160
  45.2 1.5 %collective-permute-start.17 = (bf16[400,128]{1,0:T(8,128)(2,1)S(1)}, bf16[400,128]{1,0:T(8,128)(2,1)S(1)}, u32[]{:S(2)}, u32[]{:S(2)}) collective-permute-start(bf16[400,128]{1,0:T(8,128)(2,1)S(1)} %get-tuple-element.89), channel_id=1, source_target_pairs={{0,2},{1,3},{2,0},{3,1},{4,6},{5,7},{6,4},{7,5},{8,10},{9,11},{10,... | collective-permute-start | bytes 307208 | tf_op jit(solution)/shard_map/ppermute | solution.py:160
  46.6 0.0 collective-permute-done.13.refs_1_
  46.7 1.9 %collective-permute-done.14.refs_2_ = bf16[208,128]{1,0:T(8,128)(2,1)S(1)} collective-permute-done((bf16[208,128]{1,0:T(8,128)(2,1)S(1)}, bf16[208,128]{1,0:T(8,128)(2,1)S(1)}, u32[]{:S(2)}, u32[]{:S(2)}) %collective-permute-start.14) | collective-permute-done | bytes 53280 | tf_op jit(solution)/shard_map/ppermute | solution.py:160
  48.6 0.0 collective-permute-done.15.refs_3_
  48.6 0.8 %shard_map.75 = f32[1,384,128]{2,1,0:T(8,128)} custom-call(f32[208,128]{1,0:T(8,128)S(1)} %get-tuple-element.82.refs_0_, bf16[208,128]{1,0:T(8,128)(2,1)S(1)} %collective-permute-done.13.refs_1_, bf16[208,128]{1,0:T(8,128)(2,1)S(1)} %collective-permute-done.14.refs_2_, bf16[208,128]{1,0:T(8,128)(2,1)S(1)} %collective-permute-done.15.refs_3_), custom_call_target="tpu_custom_call" | custom-call | flops 17179869184 | bytes 1024 | tf_op jit(solution)/shard_map/pallas_call | solution.py:96
  49.4 0.0 collective-permute-done.16.came_y_ref
  49.4 0.4 collective-permute-done.17.came_x_ref
  49.8 1.1 %shard_map.76 = f32[1,1536,128]{2,1,0:T(8,128)} custom-call(f32[2,400,128]{2,1,0:T(8,128)S(1)} %get-tuple-element.87.kept_ref, bf16[400,128]{1,0:T(8,128)(2,1)S(1)} %collective-permute-done.16.came_y_ref, bf16[400,128]{1,0:T(8,128)(2,1)S(1)} %collective-permute-done.17.came_x_ref), custom_call_target="tpu_custom_call" | custom-call | flops 1048576 | bytes 1024 | tf_op jit(solution)/shard_map/pallas_call | solution.py:96
Async XLA Ops:
  1.3 7.6 %copy-start = (bf16[1,4,32,12288]{3,2,1,0:T(8,128)(2,1)S(1)}, bf16[1,4,32,12288]{3,2,1,0:T(8,128)(2,1)}, u32[]{:S(2)}) copy-start(bf16[1,4,32,12288]{3,2,1,0:T(8,128)(2,1)} %refs_1_.3) | copy-start | bytes 9437188
  1.3 7.6 %copy-start.1 = (s32[4]{0:T(128)S(1)}, s32[4]{0:T(128)}, u32[]{:S(2)}) copy-start(s32[4]{0:T(128)} %order_ref.2) | copy-start | bytes 52
  3.2 14.0 %collective-permute-start = (bf16[496,128]{1,0:T(8,128)(2,1)}, bf16[496,128]{1,0:T(8,128)(2,1)S(1)}, u32[]{:S(2)}, u32[]{:S(2)}) collective-permute-start(bf16[496,128]{1,0:T(8,128)(2,1)} %get-tuple-element.50), channel_id=1, source_target_pairs={{0,16},{8,24},{16,0},{24,8},{1,17},{9,25},{17,1},{25,9},{2,18},{10... | collective-permute-start | bytes 380936 | tf_op jit(solution)/shard_map/ppermute | solution.py:160
  7.3 9.9 %collective-permute-start.1 = (bf16[496,128]{1,0:T(8,128)(2,1)}, bf16[496,128]{1,0:T(8,128)(2,1)S(1)}, u32[]{:S(2)}, u32[]{:S(2)}) collective-permute-start(bf16[496,128]{1,0:T(8,128)(2,1)} %get-tuple-element.51), channel_id=1, source_target_pairs={{0,24},{8,16},{16,8},{24,0},{1,25},{9,17},{17,9},{25,1},{2,26},{10... | collective-permute-start | bytes 380936 | tf_op jit(solution)/shard_map/ppermute | solution.py:160
  8.6 9.1 %collective-permute-start.2 = (bf16[496,128]{1,0:T(8,128)(2,1)}, bf16[496,128]{1,0:T(8,128)(2,1)S(1)}, u32[]{:S(2)}, u32[]{:S(2)}) collective-permute-start(bf16[496,128]{1,0:T(8,128)(2,1)} %get-tuple-element.52), channel_id=1, source_target_pairs={{0,8},{8,0},{16,24},{24,16},{1,9},{9,1},{17,25},{25,17},{2,10},{10... | collective-permute-start | bytes 380936 | tf_op jit(solution)/shard_map/ppermute | solution.py:160
  10.9 6.8 %copy-start.2 = (bf16[4,32,1536]{2,1,0:T(8,128)(2,1)S(1)}, bf16[4,32,1536]{2,1,0:T(8,128)(2,1)}, u32[]{:S(2)}) copy-start(bf16[4,32,1536]{2,1,0:T(8,128)(2,1)} %own_ref.1) | copy-start | bytes 1179652
  10.9 6.8 %copy-start.3 = (f32[1,6144]{1,0:T(1,128)S(1)}, f32[1,6144]{1,0:T(1,128)}, u32[]{:S(2)}) copy-start(f32[1,6144]{1,0:T(1,128)} %param.6) | copy-start | bytes 73732
  10.9 2.4 %collective-permute-start.3 = (bf16[4,2,400,128]{3,2,1,0:T(8,128)(2,1)S(1)}, bf16[4,2,400,128]{3,2,1,0:T(8,128)(2,1)S(1)}, u32[]{:S(2)}, u32[]{:S(2)}) collective-permute-start(bf16[4,2,400,128]{3,2,1,0:T(8,128)(2,1)S(1)} %shard_map.70), channel_id=1, source_target_pairs={{0,1},{1,0},{2,3},{3,2},{4,5},{5,4},{6,7},{7,6},{8,9},{9,8},{10,11... | collective-permute-start | bytes 2457608 | tf_op jit(solution)/shard_map/ppermute | solution.py:160
  13.5 12.2 %collective-permute-start.4 = (bf16[2,400,128]{2,1,0:T(8,128)(2,1)S(1)}, bf16[2,400,128]{2,1,0:T(8,128)(2,1)S(1)}, u32[]{:S(2)}, u32[]{:S(2)}) collective-permute-start(bf16[2,400,128]{2,1,0:T(8,128)(2,1)S(1)} %get-tuple-element.65), channel_id=1, source_target_pairs={{0,2},{1,3},{2,0},{3,1},{4,6},{5,7},{6,4},{7,5},{8,10},{9,11},{10,... | collective-permute-start | bytes 614408 | tf_op jit(solution)/shard_map/ppermute | solution.py:160
  15.0 10.7 %collective-permute-start.5 = (bf16[2,400,128]{2,1,0:T(8,128)(2,1)S(1)}, bf16[2,400,128]{2,1,0:T(8,128)(2,1)S(1)}, u32[]{:S(2)}, u32[]{:S(2)}) collective-permute-start(bf16[2,400,128]{2,1,0:T(8,128)(2,1)S(1)} %get-tuple-element.66), channel_id=1, source_target_pairs={{0,4},{1,5},{2,6},{3,7},{4,0},{5,1},{6,2},{7,3},{8,12},{9,13},{10,... | collective-permute-start | bytes 614408 | tf_op jit(solution)/shard_map/ppermute | solution.py:160
  25.7 5.7 %collective-permute-start.6 = (bf16[4,32,384]{2,1,0:T(8,128)(2,1)S(1)}, bf16[4,32,384]{2,1,0:T(8,128)(2,1)S(1)}, u32[]{:S(2)}, u32[]{:S(2)}) collective-permute-start(bf16[4,32,384]{2,1,0:T(8,128)(2,1)S(1)} %get-tuple-element.68), channel_id=1, source_target_pairs={{0,6},{1,7},{2,4},{3,5},{4,2},{5,3},{6,0},{7,1},{8,14},{9,15},{10,... | collective-permute-start | bytes 294920 | tf_op jit(solution)/shard_map/ppermute | solution.py:160
  28.3 5.3 %collective-permute-start.7 = (bf16[4,32,384]{2,1,0:T(8,128)(2,1)S(1)}, bf16[4,32,384]{2,1,0:T(8,128)(2,1)S(1)}, u32[]{:S(2)}, u32[]{:S(2)}) collective-permute-start(bf16[4,32,384]{2,1,0:T(8,128)(2,1)S(1)} %get-tuple-element.69), channel_id=1, source_target_pairs={{0,7},{1,6},{2,5},{3,4},{4,3},{5,2},{6,1},{7,0},{8,15},{9,14},{10,... | collective-permute-start | bytes 294920 | tf_op jit(solution)/shard_map/ppermute | solution.py:160
  28.3 7.3 %collective-permute-start.8 = (bf16[4,32,384]{2,1,0:T(8,128)(2,1)S(1)}, bf16[4,32,384]{2,1,0:T(8,128)(2,1)S(1)}, u32[]{:S(2)}, u32[]{:S(2)}) collective-permute-start(bf16[4,32,384]{2,1,0:T(8,128)(2,1)S(1)} %get-tuple-element.70), channel_id=1, source_target_pairs={{0,4},{1,5},{2,6},{3,7},{4,0},{5,1},{6,2},{7,3},{8,12},{9,13},{10,... | collective-permute-start | bytes 294920 | tf_op jit(solution)/shard_map/ppermute | solution.py:160
  28.8 7.1 %collective-permute-start.9 = (bf16[4,32,384]{2,1,0:T(8,128)(2,1)S(1)}, bf16[4,32,384]{2,1,0:T(8,128)(2,1)S(1)}, u32[]{:S(2)}, u32[]{:S(2)}) collective-permute-start(bf16[4,32,384]{2,1,0:T(8,128)(2,1)S(1)} %get-tuple-element.71), channel_id=1, source_target_pairs={{0,2},{1,3},{2,0},{3,1},{4,6},{5,7},{6,4},{7,5},{8,10},{9,11},{10,... | collective-permute-start | bytes 294920 | tf_op jit(solution)/shard_map/ppermute | solution.py:160
  29.3 8.3 %collective-permute-start.10 = (bf16[4,32,384]{2,1,0:T(8,128)(2,1)S(1)}, bf16[4,32,384]{2,1,0:T(8,128)(2,1)S(1)}, u32[]{:S(2)}, u32[]{:S(2)}) collective-permute-start(bf16[4,32,384]{2,1,0:T(8,128)(2,1)S(1)} %get-tuple-element.72), channel_id=1, source_target_pairs={{0,5},{1,4},{2,7},{3,6},{4,1},{5,0},{6,3},{7,2},{8,13},{9,12},{10,... | collective-permute-start | bytes 294920 | tf_op jit(solution)/shard_map/ppermute | solution.py:160
  31.4 6.1 %collective-permute-start.11 = (bf16[4,32,384]{2,1,0:T(8,128)(2,1)S(1)}, bf16[4,32,384]{2,1,0:T(8,128)(2,1)S(1)}, u32[]{:S(2)}, u32[]{:S(2)}) collective-permute-start(bf16[4,32,384]{2,1,0:T(8,128)(2,1)S(1)} %get-tuple-element.73), channel_id=1, source_target_pairs={{0,3},{1,2},{2,1},{3,0},{4,7},{5,6},{6,5},{7,4},{8,11},{9,10},{10,... | collective-permute-start | bytes 294920 | tf_op jit(solution)/shard_map/ppermute | solution.py:160
  33.6 4.0 %collective-permute-start.12 = (bf16[4,32,384]{2,1,0:T(8,128)(2,1)S(1)}, bf16[4,32,384]{2,1,0:T(8,128)(2,1)S(1)}, u32[]{:S(2)}, u32[]{:S(2)}) collective-permute-start(bf16[4,32,384]{2,1,0:T(8,128)(2,1)S(1)} %get-tuple-element.74), channel_id=1, source_target_pairs={{0,1},{1,0},{2,3},{3,2},{4,5},{5,4},{6,7},{7,6},{8,9},{9,8},{10,11... | collective-permute-start | bytes 294920 | tf_op jit(solution)/shard_map/ppermute | solution.py:160
  38.6 8.1 %collective-permute-start.13 = (bf16[208,128]{1,0:T(8,128)(2,1)S(1)}, bf16[208,128]{1,0:T(8,128)(2,1)S(1)}, u32[]{:S(2)}, u32[]{:S(2)}) collective-permute-start(bf16[208,128]{1,0:T(8,128)(2,1)S(1)} %get-tuple-element.83), channel_id=1, source_target_pairs={{0,16},{8,24},{16,0},{24,8},{1,17},{9,25},{17,1},{25,9},{2,18},{10... | collective-permute-start | bytes 159752 | tf_op jit(solution)/shard_map/ppermute | solution.py:160
  42.6 6.0 %collective-permute-start.14 = (bf16[208,128]{1,0:T(8,128)(2,1)S(1)}, bf16[208,128]{1,0:T(8,128)(2,1)S(1)}, u32[]{:S(2)}, u32[]{:S(2)}) collective-permute-start(bf16[208,128]{1,0:T(8,128)(2,1)S(1)} %get-tuple-element.84), channel_id=1, source_target_pairs={{0,24},{8,16},{16,8},{24,0},{1,25},{9,17},{17,9},{25,1},{2,26},{10... | collective-permute-start | bytes 159752 | tf_op jit(solution)/shard_map/ppermute | solution.py:160
  43.2 5.4 %collective-permute-start.15 = (bf16[208,128]{1,0:T(8,128)(2,1)S(1)}, bf16[208,128]{1,0:T(8,128)(2,1)S(1)}, u32[]{:S(2)}, u32[]{:S(2)}) collective-permute-start(bf16[208,128]{1,0:T(8,128)(2,1)S(1)} %get-tuple-element.85), channel_id=1, source_target_pairs={{0,8},{8,0},{16,24},{24,16},{1,9},{9,1},{17,25},{25,17},{2,10},{10... | collective-permute-start | bytes 159752 | tf_op jit(solution)/shard_map/ppermute | solution.py:160
  43.4 6.1 %collective-permute-start.16 = (bf16[400,128]{1,0:T(8,128)(2,1)S(1)}, bf16[400,128]{1,0:T(8,128)(2,1)S(1)}, u32[]{:S(2)}, u32[]{:S(2)}) collective-permute-start(bf16[400,128]{1,0:T(8,128)(2,1)S(1)} %get-tuple-element.88), channel_id=1, source_target_pairs={{0,4},{1,5},{2,6},{3,7},{4,0},{5,1},{6,2},{7,3},{8,12},{9,13},{10,... | collective-permute-start | bytes 307208 | tf_op jit(solution)/shard_map/ppermute | solution.py:160
  45.2 4.7 %collective-permute-start.17 = (bf16[400,128]{1,0:T(8,128)(2,1)S(1)}, bf16[400,128]{1,0:T(8,128)(2,1)S(1)}, u32[]{:S(2)}, u32[]{:S(2)}) collective-permute-start(bf16[400,128]{1,0:T(8,128)(2,1)S(1)} %get-tuple-element.89), channel_id=1, source_target_pairs={{0,2},{1,3},{2,0},{3,1},{4,6},{5,7},{6,4},{7,5},{8,10},{9,11},{10,... | collective-permute-start | bytes 307208 | tf_op jit(solution)/shard_map/ppermute | solution.py:160

commit v4 on v3

--- a/solution.py
+++ b/solution.py
@@ -352,14 +352,14 @@
     feats = relay(inputs, gain, repeats, me, pieces, dp_count)
     feats, came_x, came_y = lax.optimization_barrier((feats, came_x, came_y))
     gathered = [feats[0]] + [swapped(feats[mask], "dp", mask) for mask in (6, 7, 4, 2, 5, 3, 1)]
-    own, *terms = feature_terms(order, plane, gathered, micro, scale)
-    terms = [swapped(one, "section", mask) for mask, one in zip(FAR_FIRST, terms)]
-    own, first = lax.optimization_barrier((own, first))
     along_y, along_x, kept = pair_sum(first, came_x, second, came_y)
     came_y, came_x = swapped(along_y, "dp", 4), swapped(along_x, "dp", 2)
-    feature_rows = small_call(feature_sum_kernel, jax.ShapeDtypeStruct((1, 3 * BLK, BLK), jnp.float32), own, *terms, cost=1 << 34)
-    kept, feature_rows = lax.optimization_barrier((kept, feature_rows))
+    own, *terms = feature_terms(order, plane, gathered, micro, scale)
+    own, kept = lax.optimization_barrier((own, kept))
+    terms = [swapped(one, "section", mask) for mask, one in zip(FAR_FIRST, terms)]
     hidden_rows = unpacked(kept, came_y, came_x)
+    own, hidden_rows = lax.optimization_barrier((own, hidden_rows))
+    feature_rows = small_call(feature_sum_kernel, jax.ShapeDtypeStruct((1, 3 * BLK, BLK), jnp.float32), own, *terms)
     return (feature_rows, hidden_rows)
 
 

time: 50.2 us -> 50.7 us (level)
  Pallas kernels: 17.1 us -> 17.7 us
    pallas_call x1, Pallas kernels: 7.98 us -> 8.58 us  [relay(): pl.pallas_call(functools.partial(relay_kernel, sections, owners), out_sha...]
  transfers between devices with their start and end apart: 18 -> 18, of which waited for: 9 -> 7; matrix products, arithmetic and copies ran while one was open for 0% -> 0% of each run, Pallas kernels for 26% -> 29%
where the time goes in v4:
time: 50.7 us; the launch traced here: 51.2 us
  starting transfers between devices  23 us (45%)
  Pallas kernels  17.7 us (35%)
  waiting for transfers between devices  9.02 us (18%)
  between operations  1.39 us (3%)
    ppermute x18, starting transfers between devices, swapped(): lax.ppermute(shard, axis, [(i, i ^ mask) for i in range(lax.axis_size(axi...  23 us
    ppermute x18, waiting for transfers between devices, swapped(): lax.ppermute(shard, axis, [(i, i ^ mask) for i in range(lax.axis_size(axi...  9.02 us
    pallas_call x1, Pallas kernels, relay(): pl.pallas_call(functools.partial(relay_kernel, sections, owners), out_sha...  8.58 us
    pallas_call x2, Pallas kernels, hidden_terms(): pl.pallas_call(functools.partial(hidden_kernel, micro, pairs, scale), out...  3.99 us
    pallas_call x4, Pallas kernels, small_call(): pl.pallas_call(kernel, out_shape=shapes, in_specs=[VMEM_SPEC] * len(opera...  2.16 us
    pallas_call x1, Pallas kernels, messages(): pl.pallas_call(message_kernel, out_shape=(shape,) * (micro - 1), in_specs...  1.94 us
    pallas_call x1, Pallas kernels, feature_terms(): pl.pallas_call(functools.partial(feature_kernel, micro, scale), out_shape...  1.02 us
  transfers between devices with their start and end apart: 18, of which 7 were waited for; matrix products, arithmetic and copies ran while one was open for 0% of the time, Pallas kernels for 29%

profile of v4, /device:TPU:0, one launch (start us, length us, event | category | flops | bytes accessed | tf_op | source)
XLA Modules:
  0.0 51.2 jit_solution(8639652379455517431)
XLA Ops:
  1.3 0.0 copy-start
  1.3 0.0 copy-start.1
  1.3 1.9 %shard_map.68 = (bf16[496,128]{1,0:T(8,128)(2,1)}, bf16[496,128]{1,0:T(8,128)(2,1)}, bf16[496,128]{1,0:T(8,128)(2,1)}) custom-call(bf16[4,32,1536]{2,1,0:T(8,128)(2,1)} %own_ref.1, f32[48,128]{1,0:T(8,128)} %bitcast.3, s32[1]{0:T(128)S(6)} %copy.7.repeats_ref, s32[1]{0:T(128)} %bitcast.1.me_ref), custom_call_target="tpu_custom_call" | custom-call | flops 8589934592 | bytes 1048576 | tf_op jit(solution)/shard_map/pallas_call | solution.py:183
  3.2 4.0 %collective-permute-start = (bf16[496,128]{1,0:T(8,128)(2,1)}, bf16[496,128]{1,0:T(8,128)(2,1)S(1)}, u32[]{:S(2)}, u32[]{:S(2)}) collective-permute-start(bf16[496,128]{1,0:T(8,128)(2,1)} %get-tuple-element.50), channel_id=1, source_target_pairs={{0,16},{8,24},{16,0},{24,8},{1,17},{9,25},{17,1},{25,9},{2,18},{10... | collective-permute-start | bytes 380936 | tf_op jit(solution)/shard_map/ppermute | solution.py:160
  7.3 1.3 %collective-permute-start.1 = (bf16[496,128]{1,0:T(8,128)(2,1)}, bf16[496,128]{1,0:T(8,128)(2,1)S(1)}, u32[]{:S(2)}, u32[]{:S(2)}) collective-permute-start(bf16[496,128]{1,0:T(8,128)(2,1)} %get-tuple-element.51), channel_id=1, source_target_pairs={{0,24},{8,16},{16,8},{24,0},{1,25},{9,17},{17,9},{25,1},{2,26},{10... | collective-permute-start | bytes 380936 | tf_op jit(solution)/shard_map/ppermute | solution.py:160
  8.6 0.2 collective-permute-start.2
  8.9 0.0 copy-done
  8.9 0.0 copy-done.1
  8.9 2.0 %shard_map.70 = bf16[4,2,400,128]{3,2,1,0:T(8,128)(2,1)S(1)} custom-call(s32[4]{0:T(128)S(1)} %copy-done.1, s32[1]{0:T(128)S(6)} %xor.3._, bf16[1,4,32,12288]{3,2,1,0:T(8,128)(2,1)S(1)} %copy-done, bf16[1,4,32,12288]{3,2,1,0:T(8,128)(2,1)S(1)} %copy-done), custom_call_target="tpu_custom_call" | custom-call | flops 1048576 | bytes 1024 | tf_op jit(solution)/shard_map/pallas_call | solution.py:81
  10.9 0.0 copy-start.2
  10.9 0.0 copy-start.3
  10.9 0.1 collective-permute-start.3
  11.0 2.0 %shard_map.69.near_ref = bf16[4,2,400,128]{3,2,1,0:T(8,128)(2,1)S(1)} custom-call(s32[4]{0:T(128)S(1)} %copy-done.1, s32[1]{0:T(128)} %bitcast.2._, bf16[1,4,32,12288]{3,2,1,0:T(8,128)(2,1)S(1)} %copy-done, bf16[1,4,32,12288]{3,2,1,0:T(8,128)(2,1)S(1)} %copy-done), custom_call_target="tpu_custom_call" | custom-call | flops 17179869184 | bytes 1024 | tf_op jit(solution)/shard_map/pallas_call | solution.py:81
  13.0 0.3 collective-permute-done.3.came_ref
  13.3 0.2 shard_map.71
  13.5 1.6 %collective-permute-start.4 = (bf16[2,400,128]{2,1,0:T(8,128)(2,1)S(1)}, bf16[2,400,128]{2,1,0:T(8,128)(2,1)S(1)}, u32[]{:S(2)}, u32[]{:S(2)}) collective-permute-start(bf16[2,400,128]{2,1,0:T(8,128)(2,1)S(1)} %get-tuple-element.65), channel_id=1, source_target_pairs={{0,2},{1,3},{2,0},{3,1},{4,6},{5,7},{6,4},{7,5},{8,10},{9,11},{10,... | collective-permute-start | bytes 614408 | tf_op jit(solution)/shard_map/ppermute | solution.py:160
  15.0 1.5 %collective-permute-start.5 = (bf16[2,400,128]{2,1,0:T(8,128)(2,1)S(1)}, bf16[2,400,128]{2,1,0:T(8,128)(2,1)S(1)}, u32[]{:S(2)}, u32[]{:S(2)}) collective-permute-start(bf16[2,400,128]{2,1,0:T(8,128)(2,1)S(1)} %get-tuple-element.66), channel_id=1, source_target_pairs={{0,4},{1,5},{2,6},{3,7},{4,0},{5,1},{6,2},{7,3},{8,12},{9,13},{10,... | collective-permute-start | bytes 614408 | tf_op jit(solution)/shard_map/ppermute | solution.py:160
  16.6 0.1 pad_add_fusion.me_ref
  16.6 0.6 %collective-permute-done.refs_0_ = bf16[496,128]{1,0:T(8,128)(2,1)S(1)} collective-permute-done((bf16[496,128]{1,0:T(8,128)(2,1)}, bf16[496,128]{1,0:T(8,128)(2,1)S(1)}, u32[]{:S(2)}, u32[]{:S(2)}) %collective-permute-start) | collective-permute-done | bytes 127008 | tf_op jit(solution)/shard_map/ppermute | solution.py:160
  17.2 0.0 collective-permute-done.1.refs_1_
  17.2 0.5 collective-permute-done.2.refs_2_
  17.7 0.0 copy-done.2
  17.7 0.0 copy-done.3
  17.7 8.6 %shard_map.72 = (bf16[4,32,384]{2,1,0:T(8,128)(2,1)S(1)}, bf16[4,32,384]{2,1,0:T(8,128)(2,1)S(1)}, bf16[4,32,384]{2,1,0:T(8,128)(2,1)S(1)}, bf16[4,32,384]{2,1,0...) custom-call(bf16[4,32,1536]{2,1,0:T(8,128)(2,1)S(1)} %copy-done.2, ...), custom_call_target="tpu_custom_call" | custom-call | flops 2147483648 | bytes 2097152 | tf_op jit(solution)/shard_map/pallas_call | solution.py:263
  26.3 0.0 collective-permute-done.4.came_x_ref
  26.3 0.0 collective-permute-done.5.came_y_ref
  26.3 2.6 %collective-permute-start.6 = (bf16[4,32,384]{2,1,0:T(8,128)(2,1)S(1)}, bf16[4,32,384]{2,1,0:T(8,128)(2,1)S(1)}, u32[]{:S(2)}, u32[]{:S(2)}) collective-permute-start(bf16[4,32,384]{2,1,0:T(8,128)(2,1)S(1)} %get-tuple-element.68), channel_id=1, source_target_pairs={{0,6},{1,7},{2,4},{3,5},{4,2},{5,3},{6,0},{7,1},{8,14},{9,15},{10,... | collective-permute-start | bytes 294920 | tf_op jit(solution)/shard_map/ppermute | solution.py:160
  28.9 0.0 collective-permute-start.7
  28.9 0.5 collective-permute-start.8
  29.4 0.5 collective-permute-start.9
  29.9 2.2 %collective-permute-start.10 = (bf16[4,32,384]{2,1,0:T(8,128)(2,1)S(1)}, bf16[4,32,384]{2,1,0:T(8,128)(2,1)S(1)}, u32[]{:S(2)}, u32[]{:S(2)}) collective-permute-start(bf16[4,32,384]{2,1,0:T(8,128)(2,1)S(1)} %get-tuple-element.72), channel_id=1, source_target_pairs={{0,5},{1,4},{2,7},{3,6},{4,1},{5,0},{6,3},{7,2},{8,13},{9,12},{10,... | collective-permute-start | bytes 294920 | tf_op jit(solution)/shard_map/ppermute | solution.py:160
  32.0 0.0 collective-permute-done.6.refs_1_
  32.0 0.6 %collective-permute-start.11 = (bf16[4,32,384]{2,1,0:T(8,128)(2,1)S(1)}, bf16[4,32,384]{2,1,0:T(8,128)(2,1)S(1)}, u32[]{:S(2)}, u32[]{:S(2)}) collective-permute-start(bf16[4,32,384]{2,1,0:T(8,128)(2,1)S(1)} %get-tuple-element.73), channel_id=1, source_target_pairs={{0,3},{1,2},{2,1},{3,0},{4,7},{5,6},{6,5},{7,4},{8,11},{9,10},{10,... | collective-permute-start | bytes 294920 | tf_op jit(solution)/shard_map/ppermute | solution.py:160
  32.7 1.5 %collective-permute-done.7.refs_2_ = bf16[4,32,384]{2,1,0:T(8,128)(2,1)S(1)} collective-permute-done((bf16[4,32,384]{2,1,0:T(8,128)(2,1)S(1)}, bf16[4,32,384]{2,1,0:T(8,128)(2,1)S(1)}, u32[]{:S(2)}, u32[]{:S(2)}) %collective-permute-start.7) | collective-permute-done | bytes 98336 | tf_op jit(solution)/shard_map/ppermute | solution.py:160
  34.2 0.0 collective-permute-start.12
  34.2 0.1 shard_map.74
  34.3 1.9 %collective-permute-done.8.refs_3_ = bf16[4,32,384]{2,1,0:T(8,128)(2,1)S(1)} collective-permute-done((bf16[4,32,384]{2,1,0:T(8,128)(2,1)S(1)}, bf16[4,32,384]{2,1,0:T(8,128)(2,1)S(1)}, u32[]{:S(2)}, u32[]{:S(2)}) %collective-permute-start.8) | collective-permute-done | bytes 98336 | tf_op jit(solution)/shard_map/ppermute | solution.py:160
  36.1 1.5 %collective-permute-start.13 = (bf16[400,128]{1,0:T(8,128)(2,1)S(1)}, bf16[400,128]{1,0:T(8,128)(2,1)S(1)}, u32[]{:S(2)}, u32[]{:S(2)}) collective-permute-start(bf16[400,128]{1,0:T(8,128)(2,1)S(1)} %get-tuple-element.83), channel_id=1, source_target_pairs={{0,4},{1,5},{2,6},{3,7},{4,0},{5,1},{6,2},{7,3},{8,12},{9,13},{10,... | collective-permute-start | bytes 307208 | tf_op jit(solution)/shard_map/ppermute | solution.py:160
  37.6 0.0 collective-permute-done.9.refs_4_
  37.6 0.6 %collective-permute-start.14 = (bf16[400,128]{1,0:T(8,128)(2,1)S(1)}, bf16[400,128]{1,0:T(8,128)(2,1)S(1)}, u32[]{:S(2)}, u32[]{:S(2)}) collective-permute-start(bf16[400,128]{1,0:T(8,128)(2,1)S(1)} %get-tuple-element.84), channel_id=1, source_target_pairs={{0,2},{1,3},{2,0},{3,1},{4,6},{5,7},{6,4},{7,5},{8,10},{9,11},{10,... | collective-permute-start | bytes 307208 | tf_op jit(solution)/shard_map/ppermute | solution.py:160
  38.2 0.0 collective-permute-done.10.refs_5_
  38.2 0.0 collective-permute-done.11.refs_6_
  38.2 0.0 collective-permute-done.12.refs_7_
  38.3 1.0 %shard_map.73 = (f32[208,128]{1,0:T(8,128)S(1)}, bf16[208,128]{1,0:T(8,128)(2,1)S(1)}, bf16[208,128]{1,0:T(8,128)(2,1)S(1)}, bf16[208,128]{1,0:T(8,128)(2,1)S(1)}) custom-call(s32[4]{0:T(128)S(1)} %copy-done.1, s32[1]{0:T(128)} %bitcast.1.me_ref, bf16[4,32,384]{2,1,0:T(8,128)(2,1)S(1)} %get-tuple-element.67.refs_0_, ...), custom_call_target="tpu_custom_call" | custom-call | flops 2147483648 | bytes 1048576 | tf_op jit(solution)/shard_map/pallas_call | solution.py:318
  39.3 5.1 %collective-permute-start.15 = (bf16[208,128]{1,0:T(8,128)(2,1)S(1)}, bf16[208,128]{1,0:T(8,128)(2,1)S(1)}, u32[]{:S(2)}, u32[]{:S(2)}) collective-permute-start(bf16[208,128]{1,0:T(8,128)(2,1)S(1)} %get-tuple-element.86), channel_id=1, source_target_pairs={{0,16},{8,24},{16,0},{24,8},{1,17},{9,25},{17,1},{25,9},{2,18},{10... | collective-permute-start | bytes 159752 | tf_op jit(solution)/shard_map/ppermute | solution.py:160
  44.4 0.5 %collective-permute-start.16 = (bf16[208,128]{1,0:T(8,128)(2,1)S(1)}, bf16[208,128]{1,0:T(8,128)(2,1)S(1)}, u32[]{:S(2)}, u32[]{:S(2)}) collective-permute-start(bf16[208,128]{1,0:T(8,128)(2,1)S(1)} %get-tuple-element.87), channel_id=1, source_target_pairs={{0,24},{8,16},{16,8},{24,0},{1,25},{9,17},{17,9},{25,1},{2,26},{10... | collective-permute-start | bytes 159752 | tf_op jit(solution)/shard_map/ppermute | solution.py:160
  44.9 0.1 collective-permute-start.17
  45.0 0.0 collective-permute-done.13.came_y_ref
  45.0 0.0 collective-permute-done.14.came_x_ref
  45.0 1.1 %shard_map.75 = f32[1,1536,128]{2,1,0:T(8,128)} custom-call(f32[2,400,128]{2,1,0:T(8,128)S(1)} %get-tuple-element.82.kept_ref, bf16[400,128]{1,0:T(8,128)(2,1)S(1)} %collective-permute-done.13.came_y_ref, bf16[400,128]{1,0:T(8,128)(2,1)S(1)} %collective-permute-done.14.came_x_ref), custom_call_target="tpu_custom_call" | custom-call | flops 1048576 | bytes 1024 | tf_op jit(solution)/shard_map/pallas_call | solution.py:96
  46.1 1.5 %collective-permute-done.15.refs_1_ = bf16[208,128]{1,0:T(8,128)(2,1)S(1)} collective-permute-done((bf16[208,128]{1,0:T(8,128)(2,1)S(1)}, bf16[208,128]{1,0:T(8,128)(2,1)S(1)}, u32[]{:S(2)}, u32[]{:S(2)}) %collective-permute-start.15) | collective-permute-done | bytes 53280 | tf_op jit(solution)/shard_map/ppermute | solution.py:160
  47.6 2.7 %collective-permute-done.16.refs_2_ = bf16[208,128]{1,0:T(8,128)(2,1)S(1)} collective-permute-done((bf16[208,128]{1,0:T(8,128)(2,1)S(1)}, bf16[208,128]{1,0:T(8,128)(2,1)S(1)}, u32[]{:S(2)}, u32[]{:S(2)}) %collective-permute-start.16) | collective-permute-done | bytes 53280 | tf_op jit(solution)/shard_map/ppermute | solution.py:160
  50.3 0.0 collective-permute-done.17.refs_3_
  50.3 0.8 %shard_map.76 = f32[1,384,128]{2,1,0:T(8,128)} custom-call(f32[208,128]{1,0:T(8,128)S(1)} %get-tuple-element.85.refs_0_, bf16[208,128]{1,0:T(8,128)(2,1)S(1)} %collective-permute-done.15.refs_1_, bf16[208,128]{1,0:T(8,128)(2,1)S(1)} %collective-permute-done.16.refs_2_, bf16[208,128]{1,0:T(8,128)(2,1)S(1)} %collective-permute-done.17.refs_3_), custom_call_target="tpu_custom_call" | custom-call | flops 1048576 | bytes 1024 | tf_op jit(solution)/shard_map/pallas_call | solution.py:96
Async XLA Ops:
  1.3 7.6 %copy-start = (bf16[1,4,32,12288]{3,2,1,0:T(8,128)(2,1)S(1)}, bf16[1,4,32,12288]{3,2,1,0:T(8,128)(2,1)}, u32[]{:S(2)}) copy-start(bf16[1,4,32,12288]{3,2,1,0:T(8,128)(2,1)} %refs_1_.3) | copy-start | bytes 9437188
  1.3 7.6 %copy-start.1 = (s32[4]{0:T(128)S(1)}, s32[4]{0:T(128)}, u32[]{:S(2)}) copy-start(s32[4]{0:T(128)} %order_ref.2) | copy-start | bytes 52
  3.2 14.0 %collective-permute-start = (bf16[496,128]{1,0:T(8,128)(2,1)}, bf16[496,128]{1,0:T(8,128)(2,1)S(1)}, u32[]{:S(2)}, u32[]{:S(2)}) collective-permute-start(bf16[496,128]{1,0:T(8,128)(2,1)} %get-tuple-element.50), channel_id=1, source_target_pairs={{0,16},{8,24},{16,0},{24,8},{1,17},{9,25},{17,1},{25,9},{2,18},{10... | collective-permute-start | bytes 380936 | tf_op jit(solution)/shard_map/ppermute | solution.py:160
  7.3 9.9 %collective-permute-start.1 = (bf16[496,128]{1,0:T(8,128)(2,1)}, bf16[496,128]{1,0:T(8,128)(2,1)S(1)}, u32[]{:S(2)}, u32[]{:S(2)}) collective-permute-start(bf16[496,128]{1,0:T(8,128)(2,1)} %get-tuple-element.51), channel_id=1, source_target_pairs={{0,24},{8,16},{16,8},{24,0},{1,25},{9,17},{17,9},{25,1},{2,26},{10... | collective-permute-start | bytes 380936 | tf_op jit(solution)/shard_map/ppermute | solution.py:160
  8.6 9.1 %collective-permute-start.2 = (bf16[496,128]{1,0:T(8,128)(2,1)}, bf16[496,128]{1,0:T(8,128)(2,1)S(1)}, u32[]{:S(2)}, u32[]{:S(2)}) collective-permute-start(bf16[496,128]{1,0:T(8,128)(2,1)} %get-tuple-element.52), channel_id=1, source_target_pairs={{0,8},{8,0},{16,24},{24,16},{1,9},{9,1},{17,25},{25,17},{2,10},{10... | collective-permute-start | bytes 380936 | tf_op jit(solution)/shard_map/ppermute | solution.py:160
  10.9 6.8 %copy-start.2 = (bf16[4,32,1536]{2,1,0:T(8,128)(2,1)S(1)}, bf16[4,32,1536]{2,1,0:T(8,128)(2,1)}, u32[]{:S(2)}) copy-start(bf16[4,32,1536]{2,1,0:T(8,128)(2,1)} %own_ref.1) | copy-start | bytes 1179652
  10.9 6.8 %copy-start.3 = (f32[1,6144]{1,0:T(1,128)S(1)}, f32[1,6144]{1,0:T(1,128)}, u32[]{:S(2)}) copy-start(f32[1,6144]{1,0:T(1,128)} %param.6) | copy-start | bytes 73732
  10.9 2.4 %collective-permute-start.3 = (bf16[4,2,400,128]{3,2,1,0:T(8,128)(2,1)S(1)}, bf16[4,2,400,128]{3,2,1,0:T(8,128)(2,1)S(1)}, u32[]{:S(2)}, u32[]{:S(2)}) collective-permute-start(bf16[4,2,400,128]{3,2,1,0:T(8,128)(2,1)S(1)} %shard_map.70), channel_id=1, source_target_pairs={{0,1},{1,0},{2,3},{3,2},{4,5},{5,4},{6,7},{7,6},{8,9},{9,8},{10,11... | collective-permute-start | bytes 2457608 | tf_op jit(solution)/shard_map/ppermute | solution.py:160
  13.5 12.8 %collective-permute-start.4 = (bf16[2,400,128]{2,1,0:T(8,128)(2,1)S(1)}, bf16[2,400,128]{2,1,0:T(8,128)(2,1)S(1)}, u32[]{:S(2)}, u32[]{:S(2)}) collective-permute-start(bf16[2,400,128]{2,1,0:T(8,128)(2,1)S(1)} %get-tuple-element.65), channel_id=1, source_target_pairs={{0,2},{1,3},{2,0},{3,1},{4,6},{5,7},{6,4},{7,5},{8,10},{9,11},{10,... | collective-permute-start | bytes 614408 | tf_op jit(solution)/shard_map/ppermute | solution.py:160
  15.0 11.3 %collective-permute-start.5 = (bf16[2,400,128]{2,1,0:T(8,128)(2,1)S(1)}, bf16[2,400,128]{2,1,0:T(8,128)(2,1)S(1)}, u32[]{:S(2)}, u32[]{:S(2)}) collective-permute-start(bf16[2,400,128]{2,1,0:T(8,128)(2,1)S(1)} %get-tuple-element.66), channel_id=1, source_target_pairs={{0,4},{1,5},{2,6},{3,7},{4,0},{5,1},{6,2},{7,3},{8,12},{9,13},{10,... | collective-permute-start | bytes 614408 | tf_op jit(solution)/shard_map/ppermute | solution.py:160
  26.3 5.7 %collective-permute-start.6 = (bf16[4,32,384]{2,1,0:T(8,128)(2,1)S(1)}, bf16[4,32,384]{2,1,0:T(8,128)(2,1)S(1)}, u32[]{:S(2)}, u32[]{:S(2)}) collective-permute-start(bf16[4,32,384]{2,1,0:T(8,128)(2,1)S(1)} %get-tuple-element.68), channel_id=1, source_target_pairs={{0,6},{1,7},{2,4},{3,5},{4,2},{5,3},{6,0},{7,1},{8,14},{9,15},{10,... | collective-permute-start | bytes 294920 | tf_op jit(solution)/shard_map/ppermute | solution.py:160
  28.9 5.3 %collective-permute-start.7 = (bf16[4,32,384]{2,1,0:T(8,128)(2,1)S(1)}, bf16[4,32,384]{2,1,0:T(8,128)(2,1)S(1)}, u32[]{:S(2)}, u32[]{:S(2)}) collective-permute-start(bf16[4,32,384]{2,1,0:T(8,128)(2,1)S(1)} %get-tuple-element.69), channel_id=1, source_target_pairs={{0,7},{1,6},{2,5},{3,4},{4,3},{5,2},{6,1},{7,0},{8,15},{9,14},{10,... | collective-permute-start | bytes 294920 | tf_op jit(solution)/shard_map/ppermute | solution.py:160
  28.9 7.3 %collective-permute-start.8 = (bf16[4,32,384]{2,1,0:T(8,128)(2,1)S(1)}, bf16[4,32,384]{2,1,0:T(8,128)(2,1)S(1)}, u32[]{:S(2)}, u32[]{:S(2)}) collective-permute-start(bf16[4,32,384]{2,1,0:T(8,128)(2,1)S(1)} %get-tuple-element.70), channel_id=1, source_target_pairs={{0,4},{1,5},{2,6},{3,7},{4,0},{5,1},{6,2},{7,3},{8,12},{9,13},{10,... | collective-permute-start | bytes 294920 | tf_op jit(solution)/shard_map/ppermute | solution.py:160
  29.4 8.2 %collective-permute-start.9 = (bf16[4,32,384]{2,1,0:T(8,128)(2,1)S(1)}, bf16[4,32,384]{2,1,0:T(8,128)(2,1)S(1)}, u32[]{:S(2)}, u32[]{:S(2)}) collective-permute-start(bf16[4,32,384]{2,1,0:T(8,128)(2,1)S(1)} %get-tuple-element.71), channel_id=1, source_target_pairs={{0,2},{1,3},{2,0},{3,1},{4,6},{5,7},{6,4},{7,5},{8,10},{9,11},{10,... | collective-permute-start | bytes 294920 | tf_op jit(solution)/shard_map/ppermute | solution.py:160
  29.9 8.4 %collective-permute-start.10 = (bf16[4,32,384]{2,1,0:T(8,128)(2,1)S(1)}, bf16[4,32,384]{2,1,0:T(8,128)(2,1)S(1)}, u32[]{:S(2)}, u32[]{:S(2)}) collective-permute-start(bf16[4,32,384]{2,1,0:T(8,128)(2,1)S(1)} %get-tuple-element.72), channel_id=1, source_target_pairs={{0,5},{1,4},{2,7},{3,6},{4,1},{5,0},{6,3},{7,2},{8,13},{9,12},{10,... | collective-permute-start | bytes 294920 | tf_op jit(solution)/shard_map/ppermute | solution.py:160
  32.0 6.2 %collective-permute-start.11 = (bf16[4,32,384]{2,1,0:T(8,128)(2,1)S(1)}, bf16[4,32,384]{2,1,0:T(8,128)(2,1)S(1)}, u32[]{:S(2)}, u32[]{:S(2)}) collective-permute-start(bf16[4,32,384]{2,1,0:T(8,128)(2,1)S(1)} %get-tuple-element.73), channel_id=1, source_target_pairs={{0,3},{1,2},{2,1},{3,0},{4,7},{5,6},{6,5},{7,4},{8,11},{9,10},{10,... | collective-permute-start | bytes 294920 | tf_op jit(solution)/shard_map/ppermute | solution.py:160
  34.2 4.1 %collective-permute-start.12 = (bf16[4,32,384]{2,1,0:T(8,128)(2,1)S(1)}, bf16[4,32,384]{2,1,0:T(8,128)(2,1)S(1)}, u32[]{:S(2)}, u32[]{:S(2)}) collective-permute-start(bf16[4,32,384]{2,1,0:T(8,128)(2,1)S(1)} %get-tuple-element.74), channel_id=1, source_target_pairs={{0,1},{1,0},{2,3},{3,2},{4,5},{5,4},{6,7},{7,6},{8,9},{9,8},{10,11... | collective-permute-start | bytes 294920 | tf_op jit(solution)/shard_map/ppermute | solution.py:160
  36.1 8.9 %collective-permute-start.13 = (bf16[400,128]{1,0:T(8,128)(2,1)S(1)}, bf16[400,128]{1,0:T(8,128)(2,1)S(1)}, u32[]{:S(2)}, u32[]{:S(2)}) collective-permute-start(bf16[400,128]{1,0:T(8,128)(2,1)S(1)} %get-tuple-element.83), channel_id=1, source_target_pairs={{0,4},{1,5},{2,6},{3,7},{4,0},{5,1},{6,2},{7,3},{8,12},{9,13},{10,... | collective-permute-start | bytes 307208 | tf_op jit(solution)/shard_map/ppermute | solution.py:160
  37.6 7.4 %collective-permute-start.14 = (bf16[400,128]{1,0:T(8,128)(2,1)S(1)}, bf16[400,128]{1,0:T(8,128)(2,1)S(1)}, u32[]{:S(2)}, u32[]{:S(2)}) collective-permute-start(bf16[400,128]{1,0:T(8,128)(2,1)S(1)} %get-tuple-element.84), channel_id=1, source_target_pairs={{0,2},{1,3},{2,0},{3,1},{4,6},{5,7},{6,4},{7,5},{8,10},{9,11},{10,... | collective-permute-start | bytes 307208 | tf_op jit(solution)/shard_map/ppermute | solution.py:160
  39.3 8.4 %collective-permute-start.15 = (bf16[208,128]{1,0:T(8,128)(2,1)S(1)}, bf16[208,128]{1,0:T(8,128)(2,1)S(1)}, u32[]{:S(2)}, u32[]{:S(2)}) collective-permute-start(bf16[208,128]{1,0:T(8,128)(2,1)S(1)} %get-tuple-element.86), channel_id=1, source_target_pairs={{0,16},{8,24},{16,0},{24,8},{1,17},{9,25},{17,1},{25,9},{2,18},{10... | collective-permute-start | bytes 159752 | tf_op jit(solution)/shard_map/ppermute | solution.py:160
  44.4 5.9 %collective-permute-start.16 = (bf16[208,128]{1,0:T(8,128)(2,1)S(1)}, bf16[208,128]{1,0:T(8,128)(2,1)S(1)}, u32[]{:S(2)}, u32[]{:S(2)}) collective-permute-start(bf16[208,128]{1,0:T(8,128)(2,1)S(1)} %get-tuple-element.87), channel_id=1, source_target_pairs={{0,24},{8,16},{16,8},{24,0},{1,25},{9,17},{17,9},{25,1},{2,26},{10... | collective-permute-start | bytes 159752 | tf_op jit(solution)/shard_map/ppermute | solution.py:160
  44.9 5.4 %collective-permute-start.17 = (bf16[208,128]{1,0:T(8,128)(2,1)S(1)}, bf16[208,128]{1,0:T(8,128)(2,1)S(1)}, u32[]{:S(2)}, u32[]{:S(2)}) collective-permute-start(bf16[208,128]{1,0:T(8,128)(2,1)S(1)} %get-tuple-element.88), channel_id=1, source_target_pairs={{0,8},{8,0},{16,24},{24,16},{1,9},{9,1},{17,25},{25,17},{2,10},{10... | collective-permute-start | bytes 159752 | tf_op jit(solution)/shard_map/ppermute | solution.py:160
